TPU v7x, 32 devices: a whole 2x2x4 slice. The times are simulated.
32 devices in a mesh: fsdp: 8 (over z, x), tensor: 4 (over y, core).
Axes of the slice: x: 2, y: 2, z: 4, core: 2. Of those that a mesh axis runs over, the one named last changes fastest.
Arguments:
- hidden: bfloat16 [128, 28672], P('tensor', 'fsdp'), may hold values from -6 to 6
- down_weight: bfloat16 [28672, 16384], P('fsdp', 'tensor'), may hold values from -0.03125 to 0.03125
- covariance: float32 [16384, 16384], P('tensor', 'fsdp'), as said below
- keep_index: int32 [8, 8], P('fsdp'), may hold values from -1 to 15, as said below
- start_basis: float32 [16384, 512], P('fsdp'), may hold values from -6 to 6
Outputs:
- mlp_out: bfloat16 [128, 16384], P('fsdp', 'tensor')
- new_covariance: float32 [16384, 16384], P('tensor', 'fsdp')
- first_basis: float32 [16384, 512], P(('tensor', 'fsdp'))
- final_basis: float32 [16384, 512], P('fsdp')
Inputs may be any that keep to these rules, and one draw needn't show every extreme that they name: `keep_index`: row b lists first between 1 and 8 distinct positions of 0 to 15, then -1 in the remaining slots; in every draw some row lists 8 positions. covariance is exactly symmetric and positive definite.
All inputs are finite; a program needn't handle non-finite values.
Results may differ from a plain program's by a relative error of at most 0.0015.
Values may be sent and summed in bfloat16 or wider, within the bound.
No kernel may reach another device: no remote copies, remote signals or barrier semaphores. Data moves between devices by JAX's collectives and lax.ppermute only.
A program may use at most 192 MiB of HBM per device.

v0:
```python
import math

import jax
import jax.numpy as jnp
from jax import lax
from jax.sharding import PartitionSpec as P

D = 16384
TOK_DEV = 16


def broadcast(x, axis, root):
    mine = lax.axis_index(axis) == root
    return lax.psum(jnp.where(mine, x, jnp.zeros_like(x)), axis)


def gram_local(image_rows):
    return jnp.dot(
        image_rows.T,
        image_rows,
        precision=lax.Precision.HIGHEST,
        preferred_element_type=jnp.float32,
    )


def solve_rows(image_rows, lower_factor):
    return jax.scipy.linalg.solve_triangular(lower_factor, image_rows.T, lower=True).T


def body(hidden, down_weight, covariance, keep_index, start_basis):
    highest = lax.Precision.HIGHEST
    fsdp_count = lax.axis_size("fsdp")
    total_tokens = TOK_DEV * fsdp_count
    quarter = covariance.shape[0]
    block_width = covariance.shape[1]
    share_rows = quarter // fsdp_count
    group_size = fsdp_count // lax.axis_size("tensor")
    all_hidden = lax.all_gather(hidden, "tensor", axis=0, tiled=True)
    mlp_out = lax.psum_scatter(
        jnp.dot(all_hidden, down_weight, preferred_element_type=jnp.float32),
        "fsdp",
        scatter_dimension=0,
        tiled=True,
    ).astype(jnp.bfloat16)
    listed = keep_index[0]
    fsdp_index = lax.axis_index("fsdp")
    col_offset = fsdp_index % group_size * block_width
    source_index = fsdp_index // group_size
    positions = jnp.arange(mlp_out.shape[0], dtype=jnp.int32)
    marked = jnp.any(listed[:, None] == positions[None, :], axis=0).astype(jnp.bfloat16)
    row_data = lax.all_gather(mlp_out * marked[:, None], "fsdp", axis=0, tiled=True)
    column_data = broadcast(
        lax.dynamic_slice_in_dim(row_data, col_offset, block_width, 1), "tensor", source_index
    )
    update = lax.dot_general(
        row_data, column_data, (((0,), (0,)), ((), ())), preferred_element_type=jnp.float32
    )
    new_covariance = covariance + update * (1.0 / total_tokens)
    partial_image = jnp.dot(
        new_covariance, start_basis, precision=highest, preferred_element_type=jnp.float32
    )
    first_image = lax.psum(partial_image, "fsdp")
    first_gram = lax.psum(gram_local(first_image), "tensor")
    own_image = lax.dynamic_slice_in_dim(first_image, fsdp_index * share_rows, share_rows, 0)
    first_factor = jnp.linalg.cholesky(first_gram)
    first_basis = solve_rows(own_image, first_factor) * math.sqrt(D)
    carried = solve_rows(first_image, first_factor)
    partial_second = lax.dot_general(
        new_covariance,
        carried,
        (((0,), (0,)), ((), ())),
        precision=highest,
        preferred_element_type=jnp.float32,
    )
    second = lax.psum(partial_second, "tensor")
    second_gram = lax.psum(gram_local(second), "fsdp")
    final_basis = solve_rows(second, jnp.linalg.cholesky(second_gram)) * math.sqrt(D)
    return (mlp_out, new_covariance, first_basis, final_basis)


def solution(mesh):
    placed = (
        P("tensor", "fsdp"),
        P("fsdp", "tensor"),
        P("tensor", "fsdp"),
        P("fsdp", None),
        P("fsdp", None),
    )
    return jax.shard_map(
        body,
        mesh=mesh,
        in_specs=placed,
        out_specs=(
            P("fsdp", "tensor"),
            P("tensor", "fsdp"),
            P(("tensor", "fsdp"), None),
            P("fsdp", None),
        ),
        check_vma=False,
    )
```

profile of v0, /device:TPU:1, one launch (start us, length us, event | category | flops | bytes accessed | tf_op | source)
XLA Modules:
  0.0 1208.5 jit_solution(13497951138904189870)
XLA Ops:
  7.2 10.9 all_gather.6
  18.1 12.8 %fusion.100 = f32[128,4096]{1,0:T(8,128)} fusion(bf16[128,3584]{1,0:T(8,128)(2,1)S(1)} %all_gather.6, bf16[3584,4096]{1,0:T(8,128)(2,1)} %param.7), kind=kOutput, calls=%fused_computation.170 | convolution fusion | flops 3758096384 | bytes 32374784 | tf_op jit(solution)/shard_map/dot_general | solution.py:40
  31.1 66.7 %reduce-scatter.2.cloned.1.call-done = f32[16,4096]{1,0:T(8,128)} async-done(((f32[128,4096]{1,0:T(8,128)}), f32[16,4096]{1,0:T(8,128)}) %reduce-scatter.2.cloned.1.call-update) | async-done | bytes 262160 | tf_op jit(solution)/shard_map/reduce_scatter | solution.py:39
  99.6 41.0 %all-gather.2.cloned.1.call-done = bf16[128,4096]{1,0:T(8,128)(2,1)} async-done(((bf16[16,4096]{1,0:T(8,128)(2,1)}), bf16[128,4096]{1,0:T(8,128)(2,1)}) %all-gather.2.cloned.1.call-update) | async-done | bytes 1048592 | tf_op jit(solution)/shard_map/all_gather | solution.py:51
  142.6 32.4 %all-reduce.7.cloned.1.call-done = bf16[128,2048]{1,0:T(8,128)(2,1)} async-done(((bf16[128,2048]{1,0:T(8,128)(2,1)}), bf16[128,2048]{1,0:T(8,128)(2,1)}) %all-reduce.7.cloned.1.call-update) | async-done | bytes 524304 | tf_op jit(solution)/shard_map/psum | solution.py:14
  175.1 25.1 %multiply_add_fusion = f32[4096,2048]{1,0:T(8,128)} fusion(f32[4096,2048]{1,0:T(8,128)} %param.8, bf16[128,4096]{1,0:T(8,128)(2,1)} %all-gather.2.cloned.1.call-done, bf16[128,2048]{1,0:T(8,128)(2,1)} %all-reduce.7.cloned.1.call-done), kind=kOutput, calls=%fused_computation.4 | convolution fusion | flops 2164260864 | bytes 68681728 | tf_op jit(solution)/shard_map/dot_general | solution.py:55
  200.1 59.2 %fusion.101 = f32[4096,512]{1,0:T(8,128)} fusion(f32[4096,2048]{1,0:T(8,128)} %multiply_add_fusion, f32[2048,512]{1,0:T(8,128)S(1)} %copy-done.1), kind=kOutput, calls=%fused_computation.171 | convolution fusion | flops 51539607552 | bytes 46137344 | tf_op jit(solution)/shard_map/dot_general | solution.py:59
  259.4 272.0 %all-reduce.9.cloned.1.call-done = f32[4096,512]{1,0:T(8,128)} async-done(((f32[4096,512]{1,0:T(8,128)}), f32[4096,512]{1,0:T(8,128)}) %all-reduce.9.cloned.1.call-update) | async-done | bytes 8388624 | tf_op jit(solution)/shard_map/psum | solution.py:62
  531.4 18.5 %fusion.102 = f32[512,512]{0,1:T(8,128)} fusion(f32[4096,512]{1,0:T(8,128)} %all-reduce.9.cloned.1.call-done), kind=kOutput, calls=%fused_computation.172 | convolution fusion | flops 12884901888 | bytes 9437184 | tf_op jit(solution)/shard_map/dot_general | solution.py:18
  550.2 34.8 %all-reduce.11.cloned.1.call-done = f32[512,512]{0,1:T(8,128)} async-done(((f32[512,512]{0,1:T(8,128)}), f32[512,512]{0,1:T(8,128)}) %all-reduce.11.cloned.1.call-update) | async-done | bytes 1048592 | tf_op jit(solution)/shard_map/psum | solution.py:63
  588.0 11.7 cholesky.286
  599.9 9.8 custom-call.36
  610.4 11.7 cholesky.305
  622.1 10.3 custom-call.37
  633.1 11.7 cholesky.326
  644.8 9.8 custom-call.38
  655.2 11.7 cholesky.343
  679.4 39.3 %custom-call.31 = f32[4,128,128]{1,2,0:T(8,128)S(1)} custom-call(f32[4,128,128]{2,1,0:T(8,128)S(1)} %get-tuple-element.12), custom_call_target="InvertDiagBlocksLowerTriangular" | custom-call | tf_op jit(solution)/shard_map/jit(_solve_triangular)/triangular_solve | solution.py:27
  729.3 9.0 convolution_subtract_fusion
  740.2 12.2 %fusion.14 = f32[128,4096]{0,1:T(8,128)S(1)} fusion(f32[128,4096]{1,0:T(8,128)S(1)} %fusion.84, f32[128,4096]{1,0:T(8,128)S(1)} %fusion.82, f32[128,4096]{1,0:T(8,128)S(1)} %fusion.30, f32[512,4096]{0,1:T(8,128)} %bitcast.128, f32[512,512]{1,0:T(8,128)S(1)} %get-tuple-element.178), kind=kOutput, calls=%fused_computation.21 | convolution fusion | flops 2419589120 | bytes 10682368 | tf_op jit(solution)/shard_map/jit(_solve_triangular)/triangular_solve | solution.py:27
  754.4 111.0 %fusion = f32[2048,512]{1,0:T(8,128)} fusion(f32[4096,2048]{1,0:T(8,128)} %multiply_add_fusion, f32[128,4096]{1,0:T(8,128)S(1)} %fusion.86, f32[128,4096]{1,0:T(8,128)S(1)} %fusion.84, f32[128,4096]{1,0:T(8,128)S(1)} %fusion.82, f32[128,4096]{1,0:T(8,128)S(1)} %fusion.30), kind=kOutput, calls=%fused_computation.5 | convolution fusion | flops 51545899008 | bytes 46137344 | tf_op jit(solution)/shard_map/dot_general | solution.py:68
  868.2 83.3 %all-reduce.13.cloned.1.call-done = f32[2048,512]{1,0:T(8,128)} async-done(((f32[2048,512]{1,0:T(8,128)}), f32[2048,512]{1,0:T(8,128)}) %all-reduce.13.cloned.1.call-update) | async-done | bytes 4194320 | tf_op jit(solution)/shard_map/psum | solution.py:75
  951.5 11.6 fusion.103
  967.8 73.2 %all-reduce.15.cloned.1.call-done = f32[512,512]{0,1:T(8,128)} async-done(((f32[512,512]{0,1:T(8,128)}), f32[512,512]{0,1:T(8,128)}) %all-reduce.15.cloned.1.call-update) | async-done | bytes 1048592 | tf_op jit(solution)/shard_map/psum | solution.py:76
  1044.0 11.7 cholesky.358
  1055.9 9.8 custom-call.39
  1066.4 11.9 cholesky.377
  1078.3 9.8 custom-call.40
  1088.7 11.7 cholesky.398
  1100.5 9.8 custom-call.41
  1110.9 11.9 cholesky.415
  1136.2 39.3 %custom-call.32 = f32[4,128,128]{1,2,0:T(8,128)S(1)} custom-call(f32[4,128,128]{2,1,0:T(8,128)S(1)} %get-tuple-element.20), custom_call_target="InvertDiagBlocksLowerTriangular" | custom-call | tf_op jit(solution)/shard_map/jit(_solve_triangular)/triangular_solve | solution.py:27
  (119 shorter events, 98.2 us)
Async XLA Ops:
  7.2 90.6 %reduce-scatter.2.cloned.1.call-start = ((), (), s32[]{:S(2)}) async-start(), calls=%async_computation.1 | async-start | bytes 2359296 | tf_op jit(solution)/shard_map/reduce_scatter | solution.py:39
  18.1 12.9 %copy-start.2 = (s32[1,8]{1,0:T(1,128)S(1)}, s32[1,8]{1,0:T(1,128)}, u32[]{:S(2)}) copy-start(s32[1,8]{1,0:T(1,128)} %param.9) | copy-start | bytes 100
  30.9 109.7 %all-gather.2.cloned.1.call-start = ((), (), s32[]{:S(2)}) async-start(), calls=%async_computation.2 | async-start | bytes 1179648 | tf_op jit(solution)/shard_map/all_gather | solution.py:51
  99.5 75.6 %all-reduce.7.cloned.1.call-start = ((), (), s32[]{:S(2)}) async-start(), calls=%async_computation.3 | async-start | bytes 1048576 | tf_op jit(solution)/shard_map/psum | solution.py:14
  142.6 388.8 %all-reduce.9.cloned.1.call-start = ((), (), s32[]{:S(2)}) async-start(), calls=%async_computation.4 | async-start | bytes 16777216 | tf_op jit(solution)/shard_map/psum | solution.py:62
  175.1 25.1 %copy-start.1 = (f32[2048,512]{1,0:T(8,128)S(1)}, f32[2048,512]{1,0:T(8,128)}, u32[]{:S(2)}) copy-start(f32[2048,512]{1,0:T(8,128)} %param.10) | copy-start | bytes 12582916
  259.4 325.6 %all-reduce.11.cloned.1.call-start = ((), (), s32[]{:S(2)}) async-start(), calls=%async_computation.5 | async-start | bytes 2097152 | tf_op jit(solution)/shard_map/psum | solution.py:63
  549.9 401.6 %all-reduce.13.cloned.1.call-start = ((), (), s32[]{:S(2)}) async-start(), calls=%async_computation.6 | async-start | bytes 8388608 | tf_op jit(solution)/shard_map/psum | solution.py:75
  865.4 175.6 %all-reduce.15.cloned.1.call-start = ((), (), s32[]{:S(2)}) async-start(), calls=%async_computation.7 | async-start | bytes 2097152 | tf_op jit(solution)/shard_map/psum | solution.py:76
  1175.5 6.6 copy-start
Sparse Core Ops, SparseCore 0:
  31.0 66.7 reduce-scatter.1
  100.5 40.0 all-gather.1
  143.6 31.4 all-reduce.6
  259.5 271.8 all-reduce.8
  550.0 34.9 all-reduce.10
  865.5 85.9 all-reduce.12
  963.2 77.7 all-reduce.14
where the time goes:
time: 1220 us; the launch traced here: 1210 us
  waiting for transfers between devices  604 us (50%)
  matrix products  300 us (25%)
  other arithmetic  246 us (20%)
  local copies, waits for them, and re-layouts  26.8 us (2%)
  between operations  20.2 us (2%)
    psum x1, waiting for transfers between devices, body(): first_image = lax.psum(partial_image, 'fsdp')  272 us
    dot_general x1, matrix products, body(): lax.dot_general(new_covariance, carried, (((0,), (0,)), ((), ())), precis...  111 us
    psum x1, waiting for transfers between devices, body(): second = lax.psum(partial_second, 'tensor')  83.3 us
    another operation x15, other arithmetic, body(): jnp.linalg.cholesky(second_gram)  79.5 us
    another operation x5, other arithmetic, solve_rows(): jax.scipy.linalg.solve_triangular(lower_factor, image_rows.T, lower=True)  78.9 us
    another operation x14, other arithmetic, body(): first_factor = jnp.linalg.cholesky(first_gram)  78.8 us
    psum x1, waiting for transfers between devices, body(): second_gram = lax.psum(gram_local(second), 'fsdp')  73.2 us
    reduce_scatter x1, waiting for transfers between devices, body(): lax.psum_scatter(jnp.dot(all_hidden, down_weight, preferred_element_type=...  66.7 us
  transfers between devices with their start and end apart: 7, of which 7 were waited for; matrix products, arithmetic and copies ran while one was open for 1% of the time, Pallas kernels for 0%

commit v1 on v0

v1 whole, which is shorter than its diff:
```python
import math

import jax
import jax.numpy as jnp
from jax import lax
from jax.experimental import pallas as pl
from jax.experimental.pallas import tpu as pltpu
from jax.sharding import PartitionSpec as P

D = 16384
TOK_DEV = 16
HIGH = lax.Precision.HIGH
HIGHEST = lax.Precision.HIGHEST
NN = (((1,), (0,)), ((), ()))
NT = (((1,), (1,)), ((), ()))
TN = (((0,), (0,)), ((), ()))
PAD = 16
BLK = 128
TILE = 8


def base_factor(tiles_a, tiles_b, width):
    count = len(tiles_a)
    done_b = [[None] * TILE for _ in range(count)]
    for j in range(0, BLK, width):
        group, first = divmod(j, TILE)
        rows_a = [jnp.broadcast_to(tiles_a[group][first + a : first + a + 1, :], (TILE, BLK)) for a in range(width)]
        rows_b = [jnp.broadcast_to(tiles_b[group][first + a : first + a + 1, :], (TILE, BLK)) for a in range(width)]
        pivot = [[None] * width for _ in range(width)]
        for a in range(width):
            for b in range(a, width):
                pivot[a][b] = jnp.broadcast_to(rows_a[a][:, j + b : j + b + 1], (TILE, BLK))
        inverse = [None] * width
        for a in range(width):
            inverse[a] = 1.0 / pivot[a][a]
            for b in range(a + 1, width):
                factor = pivot[a][b] * inverse[a]
                for c in range(b, width):
                    pivot[b][c] = pivot[b][c] - factor * pivot[a][c]
                rows_a[b] = rows_a[b] - factor * rows_a[a]
                rows_b[b] = rows_b[b] - factor * rows_b[a]
        for a in range(width):
            done_b[group][first + a] = rows_b[a][0:1, :] * lax.rsqrt(pivot[a][a])[0:1, :]
        if j + width >= BLK:
            break
        solved_a, solved_b = [None] * width, [None] * width
        for a in reversed(range(width)):
            left, right = rows_a[a], rows_b[a]
            for b in range(a + 1, width):
                left = left - pivot[a][b] * solved_a[b]
                right = right - pivot[a][b] * solved_b[b]
            solved_a[a], solved_b[a] = left * inverse[a], right * inverse[a]
        for g in range((j + width) // TILE, count):
            left, right = tiles_a[g], tiles_b[g]
            for a in range(width):
                column = jnp.broadcast_to(tiles_a[g][:, j + a : j + a + 1], (TILE, BLK))
                left = left - column * solved_a[a]
                right = right - column * solved_b[a]
            tiles_a[g], tiles_b[g] = left, right
    return [jnp.concatenate(rows, axis=0) for rows in done_b]


def inverse_factor_kernel(gram_ref, out_ref, work, base):
    size = gram_ref.shape[0]
    blocks = size // BLK
    row = lax.broadcasted_iota(jnp.int32, (size, size), 0)
    col = lax.broadcasted_iota(jnp.int32, (size, size), 1)
    work[:, 0:size] = gram_ref[...]
    work[:, size:] = jnp.where(row == col, 1.0, 0.0)
    lane = lax.broadcasted_iota(jnp.int32, (TILE, BLK), 1)
    sub = lax.broadcasted_iota(jnp.int32, (TILE, BLK), 0)
    for k in range(blocks):
        lo, hi = k * BLK, (k + 1) * BLK
        tiles_a = [work[lo + g * TILE : lo + (g + 1) * TILE, lo:hi] for g in range(BLK // TILE)]
        tiles_b = [jnp.where(lane == sub + g * TILE, 1.0, 0.0) for g in range(BLK // TILE)]
        for g, tile in enumerate(base_factor(tiles_a, tiles_b, 4)):
            base[g * TILE : (g + 1) * TILE, :] = tile
        unit = base[...]
        if k + 1 < blocks:
            right = jnp.dot(unit, work[lo:hi, hi:size], precision=HIGHEST, preferred_element_type=jnp.float32)
        left = jnp.dot(unit, work[lo:hi, size : size + hi], precision=HIGHEST, preferred_element_type=jnp.float32)
        out_ref[lo:hi, 0:hi] = left
        if k + 1 < blocks:
            out_ref[lo:hi, hi:size] = jnp.zeros((BLK, size - hi), jnp.float32)
            tn = (((0,), (0,)), ((), ()))
            work[hi:size, hi:size] -= lax.dot_general(right, right, tn, precision=HIGHEST, preferred_element_type=jnp.float32)
            work[hi:size, size : size + hi] -= lax.dot_general(right, left, tn, precision=HIGHEST, preferred_element_type=jnp.float32)


def inverse_factor(gram):
    size = gram.shape[0]
    return pl.pallas_call(
        inverse_factor_kernel,
        out_shape=jax.ShapeDtypeStruct((size, size), jnp.float32),
        scratch_shapes=[pltpu.VMEM((size, 2 * size), jnp.float32), pltpu.VMEM((BLK, BLK), jnp.float32)],
        compiler_params=pltpu.CompilerParams(vmem_limit_bytes=16 * 1024 * 1024),
        name="inverse_factor",
    )(gram)


def dot(left, right, dims=NN, precision=HIGH):
    return lax.dot_general(left, right, dims, precision=precision, preferred_element_type=jnp.float32)


def swap(x, axis, bit):
    return lax.ppermute(x, axis, [(i, i ^ bit) for i in range(lax.axis_size(axis))])


def bits_of(axis):
    return [1 << b for b in range(lax.axis_size(axis).bit_length() - 1)]


def pack(x):
    top = jnp.max(jnp.abs(x))
    power = jnp.where(top > 0, jnp.ceil(jnp.log2(top)), 0.0)
    power = jnp.maximum(power, -100.0) - 15.0
    values = (x * jnp.exp2(-power)).astype(jnp.float16)
    return jnp.concatenate([values, jnp.full((PAD, x.shape[1]), power, jnp.float16)], axis=0)


def unpack(message):
    rows = message.shape[0] - PAD
    power = message[rows, 0].astype(jnp.float32)
    return message[:rows].astype(jnp.float32) * jnp.exp2(power)


def block(x, index, size, axis):
    return lax.dynamic_slice_in_dim(x, index * size, size, axis)


def gather_relative(x, axis, bits):
    held = {0: x}
    for bit in bits:
        for m in sorted(held):
            held[m ^ bit] = swap(held[m], axis, bit)
    return held


def gather_rows(x, axis, bits):
    held, order = x[None], [0]
    for bit in bits:
        held = jnp.concatenate([held, swap(held, axis, bit)], axis=0)
        order = order + [m ^ bit for m in order]
    place = sorted(range(len(order)), key=lambda i: order[i])
    return jnp.stack([held[i] for i in place])


def sum_rows(x, axis, bits, relative):
    for bit in bits:
        other = swap(x, axis, bit)
        if relative:
            other = jnp.stack([other[m ^ bit] for m in range(x.shape[0])])
        x = x + other
    return x


def sum_square(x):
    f_bits, t_bits = bits_of("fsdp"), bits_of("tensor")
    halved = [("tensor", bit) for bit in t_bits] + [("fsdp", bit) for bit in f_bits[:1]]
    for axis, bit in halved:
        half = x.shape[0] // 2
        side = (lax.axis_index(axis) & bit) // bit
        x = block(x, side, half, 0) + swap(block(x, 1 - side, half, 0), axis, bit)
    for bit in f_bits[1:]:
        x = x + swap(x, "fsdp", bit)
    for axis, bit in reversed(halved):
        other = swap(x, axis, bit)
        side = (lax.axis_index(axis) & bit) // bit
        x = jnp.where(side == 0, jnp.concatenate([x, other]), jnp.concatenate([other, x]))
    return x


def scatter_tokens(partial, bits, row_of):
    held = {m: row_of(partial, m) for m in range(lax.axis_size("fsdp"))}
    for bit in bits:
        sent = [m for m in sorted(held) if m & bit]
        came = swap(jnp.stack([held[m] for m in sent]), "fsdp", bit)
        for at, m in enumerate(sent):
            held[m ^ bit] = held[m ^ bit] + came[at]
            del held[m]
    return held[0]


def body(hidden, down_weight, covariance, keep_index, start_basis):
    f_count, t_count = lax.axis_size("fsdp"), lax.axis_size("tensor")
    f, t = lax.axis_index("fsdp"), lax.axis_index("tensor")
    f_bits, t_bits = bits_of("fsdp"), bits_of("tensor")
    quarter, width = covariance.shape
    rank = start_basis.shape[1]
    share = quarter // f_count
    group = f_count // t_count
    part = width // t_count
    root = math.sqrt(D)

    tokens = gather_rows(hidden, "tensor", t_bits[::-1])
    tokens = tokens.reshape(-1, hidden.shape[1])
    partial_out = jnp.dot(tokens, down_weight, preferred_element_type=jnp.float32)

    def token_rows(x, m):
        owner = f ^ m
        return block(x, ((owner // group) ^ t) * group + owner % group, TOK_DEV, 0)

    half = partial_out.shape[1] // 2
    swapped = f_bits[1:2] + f_bits[:1] + f_bits[2:]
    mlp_out = jnp.concatenate(
        [
            scatter_tokens(partial_out[:, :half], f_bits, token_rows),
            scatter_tokens(partial_out[:, half:], swapped, token_rows),
        ],
        axis=1,
    ).astype(jnp.bfloat16)

    positions = jnp.arange(TOK_DEV, dtype=jnp.int32)
    picks = (keep_index[0][:, None] == positions[None, :]).astype(jnp.bfloat16)
    kept = jnp.dot(picks, mlp_out, preferred_element_type=jnp.float32).astype(jnp.bfloat16)
    slots = kept.shape[0]
    row_data = gather_rows(kept, "fsdp", f_bits[::-1])
    column_data = block(row_data, f % group, width, 2) * (t == f // group).astype(jnp.bfloat16)
    for bit in t_bits:
        column_data = column_data + swap(column_data, "tensor", bit)
    row_data = row_data.reshape(f_count * slots, quarter)
    column_flat = column_data.reshape(f_count * slots, width)
    per_token = 1.0 / (TOK_DEV * f_count)

    held = {}
    for m in sorted(range(f_count), key=lambda m: (-(m & 1), -m)):
        held[m] = dot(block(covariance, f ^ m, share, 0), start_basis)
    for bit in f_bits:
        for m in sorted((m for m in held if m & bit), key=lambda m: -m):
            came = unpack(swap(pack(held.pop(m)), "fsdp", bit))
            held[m ^ bit] = held[m ^ bit] + came
    raw = held[0].T

    kept_start = dot(column_flat.astype(jnp.float32), start_basis).reshape(f_count, slots, rank)
    kept_start = sum_rows(kept_start, "fsdp", f_bits, True).reshape(f_count * slots, rank) * per_token

    def kept_part(m):
        return dot(kept_start, block(row_data, f ^ m, share, 1).astype(jnp.float32), TN)

    own = raw + kept_part(0)
    pieces = gather_relative(pack(raw), "fsdp", f_bits[::-1])

    total = dot(own, block(covariance, f, share, 0))
    for m in range(1, f_count):
        image = unpack(pieces[m]) + kept_part(m)
        total = total + dot(image, block(covariance, f ^ m, share, 0))
    seconds = {m: block(total, t ^ m, part, 1) for m in range(t_count)}
    for at, bit in enumerate(t_bits):
        for m in sorted((m for m in seconds if m & bit), key=lambda m: -m):
            sent = seconds.pop(m)
            came = swap(sent, "tensor", bit) if at == 0 else unpack(swap(pack(sent), "tensor", bit))
            seconds[m ^ bit] = seconds[m ^ bit] + came
    kept_image = dot(block(row_data, f, share, 1).astype(jnp.float32), own, NT)
    kept_image = kept_image.reshape(f_count, slots, rank)
    kept_image = sum_rows(kept_image, "tensor", t_bits, False)
    kept_image = sum_rows(kept_image, "fsdp", f_bits, True).reshape(f_count * slots, rank) * per_token
    second = seconds[0] + dot(kept_image, block(column_flat, t, part, 1).astype(jnp.float32), TN)

    first_inverse = inverse_factor(sum_square(dot(own, own, NT, HIGHEST)))
    first_basis = lax.dot_general(
        own, first_inverse, (((0,), (1,)), ((), ())), precision=HIGH, preferred_element_type=jnp.float32
    ) * root

    second = dot(first_inverse, second)
    last_inverse = inverse_factor(sum_square(dot(second, second, NT, HIGHEST)))
    parts = gather_rows(second.T, "tensor", t_bits[::-1])
    image = jnp.concatenate([lax.dynamic_index_in_dim(parts, t ^ m, 0, False) for m in range(t_count)])
    final_basis = dot(image, last_inverse, NT) * root

    update = lax.dot_general(row_data, column_flat, TN, preferred_element_type=jnp.float32)
    new_covariance = covariance + update * per_token
    return (mlp_out, new_covariance, first_basis, final_basis)


def solution(mesh):
    placed = (
        P("tensor", "fsdp"),
        P("fsdp", "tensor"),
        P("tensor", "fsdp"),
        P("fsdp", None),
        P("fsdp", None),
    )
    return jax.shard_map(
        body,
        mesh=mesh,
        in_specs=placed,
        out_specs=(
            P("fsdp", "tensor"),
            P("tensor", "fsdp"),
            P(("tensor", "fsdp"), None),
            P("fsdp", None),
        ),
        check_vma=False,
    )
```

time: 1220 us -> 557 us (0.46)
  waiting for transfers between devices: 604 us -> 132 us
  other arithmetic: 246 us -> 33.1 us
  matrix products: 300 us -> 192 us
  starting transfers between devices: 0.51 us -> 67.2 us
  Pallas kernels: 0 us -> 59.2 us
    psum x5 -> x0, waiting for transfers between devices: 496 us -> none  [the longest x1 272 us: body(): first_image = lax.psum(partial_image, 'fsdp')]
    another operation x34 -> x12, other arithmetic: 237 us -> 8.83 us  [the longest x8 5.05 us: scatter_tokens(): came = swap(jnp.stack([held[m] for m in sent]), 'fsdp', bit)]
    ppermute x0 -> x56, waiting for transfers between devices: none -> 132 us  [swap(): lax.ppermute(x, axis, [(i, i ^ bit) for i in range(lax.axis_size(axis))])]
    ppermute x0 -> x56, starting transfers between devices: none -> 67.2 us  [swap(): lax.ppermute(x, axis, [(i, i ^ bit) for i in range(lax.axis_size(axis))])]
    reduce_scatter x1 -> x0, waiting for transfers between devices: 66.7 us -> none  [body(): lax.psum_scatter(jnp.dot(all_hidden, down_weight, preferred_element_type=...]
    another operation x33 -> x0, matrix products: 62 us -> none  [the longest x21 58.2 us: solve_rows(): jax.scipy.linalg.solve_triangular(lower_factor, image_rows.T, lower=True)]
    pallas_call x0 -> x2, Pallas kernels: none -> 59.2 us  [inverse_factor(): pl.pallas_call(inverse_factor_kernel, out_shape=jax.ShapeDtypeStruct((siz...]
    dot_general x6 -> x35, matrix products: 238 us -> 192 us  [the longest x31 151 us: dot(): lax.dot_general(left, right, dims, precision=precision, preferred_element...]
  transfers between devices with their start and end apart: 7 -> 56, of which waited for: 7 -> 24; matrix products, arithmetic and copies ran while one was open for 1% -> 43% of each run, Pallas kernels for 0% -> 11%
where the time goes in v1:
time: 557 us; the launch traced here: 547 us
  matrix products  192 us (34%)
  waiting for transfers between devices  132 us (24%)
  starting transfers between devices  67.2 us (12%)
  Pallas kernels  59.2 us (11%)
  local copies, waits for them, and re-layouts  39 us (7%)
  other arithmetic  33.1 us (6%)
  between operations  25.2 us (5%)
    dot_general x31, matrix products, dot(): lax.dot_general(left, right, dims, precision=precision, preferred_element...  151 us
    ppermute x56, waiting for transfers between devices, swap(): lax.ppermute(x, axis, [(i, i ^ bit) for i in range(lax.axis_size(axis))])  132 us
    ppermute x56, starting transfers between devices, swap(): lax.ppermute(x, axis, [(i, i ^ bit) for i in range(lax.axis_size(axis))])  67.2 us
    pallas_call x2, Pallas kernels, inverse_factor(): pl.pallas_call(inverse_factor_kernel, out_shape=jax.ShapeDtypeStruct((siz...  59.2 us
    dot_general x1, matrix products, body(): lax.dot_general(row_data, column_flat, TN, preferred_element_type=jnp.flo...  25 us
    slice x15, local copies, waits for them, and re-layouts, unpack(): power = message[rows, 0].astype(jnp.float32)  15.2 us
    dot_general x1, matrix products, body(): jnp.dot(tokens, down_weight, preferred_element_type=jnp.float32)  12.2 us
  transfers between devices with their start and end apart: 56, of which 24 were waited for; matrix products, arithmetic and copies ran while one was open for 43% of the time, Pallas kernels for 11%

profile of v1, /device:TPU:1, one launch (start us, length us, event | category | flops | bytes accessed | tf_op | source)
XLA Modules:
  0.0 547.4 jit_solution(12664684853323730337)
XLA Ops:
  2.8 7.7 %abs_reduce_fusion.4 = (f32[]{:T(128)}, f32[512,512]{1,0:T(8,128)S(1)}) fusion(f32[2048,512]{1,0:T(8,128)} %param.9, f32[4096,2048]{1,0:T(8,128)} %param.7, s32[]{:T(128)S(6)} %select_n.324), kind=kOutput, calls=%fused_computation.104 | convolution fusion | flops 3221749760 | bytes 9437192 | tf_op jit(solution)/shard_map/dot_general | solution.py:102
  14.0 7.6 %abs_reduce_fusion.6 = (f32[]{:T(128)}, f32[512,512]{1,0:T(8,128)S(1)}) fusion(f32[2048,512]{1,0:T(8,128)} %param.9, f32[4096,2048]{1,0:T(8,128)} %param.7, s32[]{:T(128)S(6)} %select_n.320), kind=kOutput, calls=%fused_computation.111 | convolution fusion | flops 3221749760 | bytes 9437192 | tf_op jit(solution)/shard_map/dot_general | solution.py:102
  23.6 7.7 %abs_reduce_fusion.7 = (f32[]{:T(128)}, f32[512,512]{1,0:T(8,128)S(1)}) fusion(f32[2048,512]{1,0:T(8,128)} %param.9, f32[4096,2048]{1,0:T(8,128)} %param.7, s32[]{:T(128)S(6)} %select_n.317), kind=kOutput, calls=%fused_computation.114 | convolution fusion | flops 3221749760 | bytes 9437192 | tf_op jit(solution)/shard_map/dot_general | solution.py:102
  34.7 7.6 %abs_reduce_fusion.3 = (f32[]{:T(128)}, f32[512,512]{1,0:T(8,128)S(1)}) fusion(f32[2048,512]{1,0:T(8,128)} %param.9, f32[4096,2048]{1,0:T(8,128)} %param.7, s32[]{:T(128)S(6)} %select_n.327), kind=kOutput, calls=%fused_computation.102 | convolution fusion | flops 3221749760 | bytes 9437192 | tf_op jit(solution)/shard_map/dot_general | solution.py:102
  45.2 6.6 %fusion.42 = f32[512,512]{0,1:T(8,128)S(1)} fusion(f32[2048,512]{1,0:T(8,128)} %param.9, f32[4096,2048]{1,0:T(8,128)} %param.7, s32[]{:T(128)S(6)} %select_n.316), kind=kOutput, calls=%fused_computation.46 | convolution fusion | flops 3221225472 | bytes 9437188 | tf_op jit(solution)/shard_map/dot_general | solution.py:102
  56.3 7.9 %abs_reduce_fusion.5 = (f32[]{:T(128)}, f32[512,512]{1,0:T(8,128)S(1)}) fusion(f32[]{:T(128)} %bitcast.34, f16[528,512]{1,0:T(8,128)(2,1)S(1)} %collective-permute-done.14, f32[2048,512]{1,0:T(8,128)} %param.9, f32[4096,2048]{1,0:T(8,128)} %param.7, s32[]{:T(128)S(6)} %select_n.319), kind=kOutput, calls=%fused_computation.108 | convolution fusion | flops 3222536192 | bytes 9961992 | tf_op jit(solution)/shard_map/dot_general | solution.py:102
  66.9 7.7 %abs_reduce_fusion.2 = (f32[]{:T(128)}, f32[512,512]{1,0:T(8,128)S(1)}) fusion(f32[]{:T(128)} %bitcast.37, f16[528,512]{1,0:T(8,128)(2,1)} %copy-done.6, f32[2048,512]{1,0:T(8,128)} %param.9, f32[4096,2048]{1,0:T(8,128)} %param.7, s32[]{:T(128)S(6)} %select_n.326), kind=kOutput, calls=%fused_computation.99 | convolution fusion | flops 3222536192 | bytes 9961992 | tf_op jit(solution)/shard_map/dot_general | solution.py:102
  86.8 12.2 %fusion.183 = f32[128,4096]{1,0:T(8,128)S(1)} fusion(bf16[128,3584]{1,0:T(8,128)(2,1)S(1)} %bitcast.197, bf16[3584,4096]{1,0:T(8,128)(2,1)} %param.6), kind=kOutput, calls=%fused_computation.296 | convolution fusion | flops 3758096384 | bytes 32374784 | tf_op jit(solution)/shard_map/dot_general | solution.py:197
  108.6 8.4 %collective-permute-done.5 = f32[4,16,2048]{2,1,0:T(8,128)} collective-permute-done((f32[4,16,2048]{2,1,0:T(8,128)}, f32[4,16,2048]{2,1,0:T(8,128)}, u32[]{:S(2)}, u32[]{:S(2)}) %collective-permute-start.5) | collective-permute-done | bytes 524320 | tf_op jit(solution)/shard_map/ppermute | solution.py:106
  133.9 6.2 %collective-permute-done.4 = f32[1,16,2048]{2,1,0:T(8,128)S(1)} collective-permute-done((f32[1,16,2048]{2,1,0:T(8,128)S(1)}, f32[1,16,2048]{2,1,0:T(8,128)S(1)}, u32[]{:S(2)}, u32[]{:S(2)}) %collective-permute-start.4) | collective-permute-done | bytes 131104 | tf_op jit(solution)/shard_map/ppermute | solution.py:106
  141.9 6.6 %abs_reduce_fusion.1 = (f32[]{:T(128)}, f32[512,512]{1,0:T(8,128)S(1)}) fusion(f32[]{:T(128)} %bitcast.38, f16[528,512]{1,0:T(8,128)(2,1)} %collective-permute-done.18, f32[]{:T(128)} %bitcast.36, f16[528,512]{1,0:T(8,128)(2,1)} %collective-permute-done.16, f32[2048,512]{1,0:T(8,128)S(1)} %copy-done, f32[4096,2048]{1,0:T(8,128)} %param.7, s32[]{:T(128)S(6)} %select_n.323), kind=kOutput, calls=%fused_computation.96 | convolution fusion | flops 3223322624 | bytes 10486792 | tf_op jit(solution)/shard_map/dot_general | solution.py:102
  165.2 21.6 %collective-permute-done.19 = f16[528,512]{1,0:T(8,128)(2,1)} collective-permute-done((f16[528,512]{1,0:T(8,128)(2,1)}, f16[528,512]{1,0:T(8,128)(2,1)}, u32[]{:S(2)}, u32[]{:S(2)}) %collective-permute-start.19) | collective-permute-done | bytes 540704 | tf_op jit(solution)/shard_map/ppermute | solution.py:106
  219.3 20.3 %collective-permute-done.34 = f16[528,512]{1,0:T(8,128)(2,1)} collective-permute-done((f16[528,512]{1,0:T(8,128)(2,1)S(1)}, f16[528,512]{1,0:T(8,128)(2,1)}, u32[]{:S(2)}, u32[]{:S(2)}) %collective-permute-start.34) | collective-permute-done | bytes 540704 | tf_op jit(solution)/shard_map/ppermute | solution.py:106
  248.5 8.6 %collective-permute-done.36 = f16[528,512]{1,0:T(8,128)(2,1)} collective-permute-done((f16[528,512]{1,0:T(8,128)(2,1)}, f16[528,512]{1,0:T(8,128)(2,1)}, u32[]{:S(2)}, u32[]{:S(2)}) %collective-permute-start.36) | collective-permute-done | bytes 540704 | tf_op jit(solution)/shard_map/ppermute | solution.py:106
  272.9 7.6 %fusion.40 = f32[512,2048]{1,0:T(8,128)} fusion(f32[512,512]{1,0:T(8,128)S(1)} %convolution_add_fusion, f32[4096,2048]{1,0:T(8,128)} %param.7, s32[]{:T(128)S(6)} %select_n.316), kind=kOutput, calls=%fused_computation.44 | convolution fusion | flops 3221225472 | bytes 9437188 | tf_op jit(solution)/shard_map/dot_general | solution.py:102
  283.0 7.9 %fusion.36 = f32[512,2048]{1,0:T(8,128)} fusion(f32[4096,2048]{1,0:T(8,128)} %param.7, s32[]{:T(128)S(6)} %select_n.317, f32[512,512]{1,0:T(8,128)S(1)} %fusion.138, f16[528,512]{1,0:T(8,128)(2,1)} %collective-permute-done.31, f32[]{:T(128)} %bitcast.44), kind=kOutput, calls=%fused_computation.40 | convolution fusion | flops 3222011904 | bytes 9961988 | tf_op jit(solution)/shard_map/dot_general | solution.py:102
  290.9 8.0 %fusion.32 = f32[512,2048]{1,0:T(8,128)} fusion(f32[4096,2048]{1,0:T(8,128)} %param.7, s32[]{:T(128)S(6)} %select_n.319, f32[512,512]{1,0:T(8,128)S(1)} %fusion.136, f16[528,512]{1,0:T(8,128)(2,1)} %collective-permute-done.32, f32[]{:T(128)} %bitcast.45), kind=kOutput, calls=%fused_computation.36 | convolution fusion | flops 3222011904 | bytes 9961988 | tf_op jit(solution)/shard_map/dot_general | solution.py:102
  298.9 7.8 %fusion.28 = f32[512,2048]{1,0:T(8,128)} fusion(f32[4096,2048]{1,0:T(8,128)} %param.7, s32[]{:T(128)S(6)} %select_n.320, f32[512,512]{1,0:T(8,128)S(1)} %fusion.134, f16[528,512]{1,0:T(8,128)(2,1)} %collective-permute-done.33, f32[]{:T(128)} %bitcast.46), kind=kOutput, calls=%fused_computation.32 | convolution fusion | flops 3222011904 | bytes 9961988 | tf_op jit(solution)/shard_map/dot_general | solution.py:102
  306.7 8.3 %fusion.24 = f32[512,2048]{1,0:T(8,128)} fusion(f32[4096,2048]{1,0:T(8,128)} %param.7, s32[]{:T(128)S(6)} %select_n.323, f32[512,512]{1,0:T(8,128)S(1)} %fusion.132, f16[528,512]{1,0:T(8,128)(2,1)} %collective-permute-done.34, f32[]{:T(128)} %bitcast.47), kind=kOutput, calls=%fused_computation.28 | convolution fusion | flops 3222011904 | bytes 9961988 | tf_op jit(solution)/shard_map/dot_general | solution.py:102
  315.1 7.9 %fusion.20 = f32[512,2048]{1,0:T(8,128)} fusion(f32[4096,2048]{1,0:T(8,128)} %param.7, s32[]{:T(128)S(6)} %select_n.324, f32[512,512]{1,0:T(8,128)S(1)} %fusion.130, f16[528,512]{1,0:T(8,128)(2,1)} %collective-permute-done.35, f32[]{:T(128)} %bitcast.48), kind=kOutput, calls=%fused_computation.24 | convolution fusion | flops 3222011904 | bytes 9961988 | tf_op jit(solution)/shard_map/dot_general | solution.py:102
  323.0 7.9 %fusion.16 = f32[512,2048]{1,0:T(8,128)} fusion(f32[4096,2048]{1,0:T(8,128)} %param.7, s32[]{:T(128)S(6)} %select_n.326, f32[512,512]{1,0:T(8,128)S(1)} %fusion.128, f16[528,512]{1,0:T(8,128)(2,1)} %collective-permute-done.36, f32[]{:T(128)} %bitcast.49), kind=kOutput, calls=%fused_computation.20 | convolution fusion | flops 3222011904 | bytes 9961988 | tf_op jit(solution)/shard_map/dot_general | solution.py:102
  337.1 15.6 %add_add_fusion = f32[512,2048]{1,0:T(8,128)S(1)} fusion(f32[512,2048]{1,0:T(8,128)} %fusion.16, f32[512,2048]{1,0:T(8,128)} %fusion.20, f32[512,2048]{1,0:T(8,128)} %fusion.24, f32[512,2048]{1,0:T(8,128)} %fusion.28, f32[512,2048]{1,0:T(8,128)} %fusion.32, f32[512,2048]{1,0:T(8,128)} %fusion.40, f32[512,2048]{1,0:T(8,128)} %fusion.36, ...), kind=kOutput, calls=%fused_computation.15 | convolution fusion | flops 3229351936 | bytes 39322116 | tf_op jit(solution)/shard_map/dot_general | solution.py:102
  355.1 7.7 %collective-permute-done.24 = f32[128,512]{1,0:T(8,128)S(1)} collective-permute-done((f32[128,512]{1,0:T(8,128)S(1)}, f32[128,512]{1,0:T(8,128)S(1)}, u32[]{:S(2)}, u32[]{:S(2)}) %collective-permute-start.24) | collective-permute-done | bytes 262176 | tf_op jit(solution)/shard_map/ppermute | solution.py:106
  373.5 5.4 collective-permute-done.27
  386.8 7.3 %collective-permute-start.38 = (f32[512,512]{1,0:T(8,128)S(1)}, f32[512,512]{1,0:T(8,128)S(1)}, u32[]{:S(2)}, u32[]{:S(2)}) collective-permute-start(f32[512,512]{1,0:T(8,128)S(1)} %get-tuple-element.11), channel_id=1, source_target_pairs={{0,1},{1,0},{2,3},{3,2},{4,5},{5,4},{6,7},{7,6},{8,9},{9,8},{10,11... | collective-permute-start | bytes 3145736 | tf_op jit(solution)/shard_map/ppermute | solution.py:106
  401.6 29.7 %inverse_factor.2 = f32[512,512]{1,0:T(8,128)S(1)} custom-call(f32[512,512]{1,0:T(8,128)S(1)} %maximum_select_fusion.gram_ref), custom_call_target="tpu_custom_call" | custom-call | tf_op jit(solution)/shard_map/inverse_factor/pallas_call | solution.py:92
  442.4 6.1 %collective-permute-done.49 = f32[128,512]{1,0:T(8,128)S(1)} collective-permute-done((f32[128,512]{1,0:T(8,128)S(1)}, f32[128,512]{1,0:T(8,128)S(1)}, u32[]{:S(2)}, u32[]{:S(2)}) %collective-permute-start.49) | collective-permute-done | bytes 262176 | tf_op jit(solution)/shard_map/ppermute | solution.py:106
  452.9 4.2 collective-permute-done.51
  457.4 5.6 %collective-permute-done.52 = f32[64,512]{1,0:T(8,128)S(1)} collective-permute-done((f32[64,512]{1,0:T(8,128)S(1)}, f32[64,512]{1,0:T(8,128)S(1)}, u32[]{:S(2)}, u32[]{:S(2)}) %collective-permute-start.52) | collective-permute-done | bytes 131104 | tf_op jit(solution)/shard_map/ppermute | solution.py:106
  481.2 25.0 %fusion = f32[4096,2048]{1,0:T(8,128)} fusion(f32[4096,2048]{1,0:T(8,128)} %param.7, bf16[8,8,4096]{2,1,0:T(8,128)(2,1)S(1)} %copy-done.4, bf16[8,8,2048]{2,1,0:T(8,128)(2,1)S(1)} %fusion.216, bf16[8,8,2048]{2,1,0:T(8,128)(2,1)} %collective-permute-done.12), kind=kOutput, calls=%fused_computation.1 | convolution fusion | flops 1090650112 | bytes 68157440 | tf_op jit(solution)/shard_map/dot_general | solution.py:270
  509.2 29.5 %inverse_factor.3 = f32[512,512]{1,0:T(8,128)S(1)} custom-call(f32[512,512]{1,0:T(8,128)S(1)} %maximum_select_fusion.1.gram_ref), custom_call_target="tpu_custom_call" | custom-call | tf_op jit(solution)/shard_map/inverse_factor/pallas_call | solution.py:92
  541.1 5.9 %fusion.44 = f32[2048,512]{1,0:T(8,128)} fusion(f32[512,512]{1,0:T(8,128)S(1)} %inverse_factor.3, f32[512,512]{1,0:T(8,128)S(1)} %get-tuple-element.7, f32[512,512]{1,0:T(8,128)S(1)} %get-tuple-element.8, f32[512,512]{1,0:T(8,128)S(1)} %get-tuple-element.9, f32[512,512]{1,0:T(8,128)S(1)} %get-tuple-element.6), kind=kOutput, calls=%fused_computation.48 | convolution fusion | flops 3225419776 | bytes 9437184 | tf_op jit(solution)/shard_map/dot_general | solution.py:102
  (267 shorter events, 188.1 us)
Async XLA Ops:
  0.6 51.5 %collective-permute-start = (bf16[1,32,3584]{2,1,0:T(8,128)(2,1)}, bf16[1,32,3584]{2,1,0:T(8,128)(2,1)S(1)}, u32[]{:S(2)}, u32[]{:S(2)}) collective-permute-start(bf16[1,32,3584]{2,1,0:T(8,128)(2,1)} %bitcast.207), channel_id=1, source_target_pairs={{0,2},{1,3},{2,0},{3,1},{4,6},{5,7},{6,4},{7,5},{8,10},{9,11},{10,... | collective-permute-start | bytes 688136 | tf_op jit(solution)/shard_map/ppermute | solution.py:106
  12.8 63.1 %collective-permute-start.16 = (f16[528,512]{1,0:T(8,128)(2,1)}, f16[528,512]{1,0:T(8,128)(2,1)}, u32[]{:S(2)}, u32[]{:S(2)}) collective-permute-start(f16[528,512]{1,0:T(8,128)(2,1)} %concatenate.90), channel_id=1, source_target_pairs={{0,4},{4,0},{8,12},{12,8},{16,20},{20,16},{24,28},{28,24},{1,5},{5... | collective-permute-start | bytes 1622024 | tf_op jit(solution)/shard_map/ppermute | solution.py:106
  23.1 31.9 %collective-permute-start.14 = (f16[528,512]{1,0:T(8,128)(2,1)S(1)}, f16[528,512]{1,0:T(8,128)(2,1)S(1)}, u32[]{:S(2)}, u32[]{:S(2)}) collective-permute-start(f16[528,512]{1,0:T(8,128)(2,1)S(1)} %concatenate.88), channel_id=1, source_target_pairs={{0,4},{4,0},{8,12},{12,8},{16,20},{20,16},{24,28},{28,24},{1,5},{5... | collective-permute-start | bytes 1622024 | tf_op jit(solution)/shard_map/ppermute | solution.py:106
  33.7 47.2 %collective-permute-start.13 = (f16[528,512]{1,0:T(8,128)(2,1)}, f16[528,512]{1,0:T(8,128)(2,1)}, u32[]{:S(2)}, u32[]{:S(2)}) collective-permute-start(f16[528,512]{1,0:T(8,128)(2,1)} %concatenate.87), channel_id=1, source_target_pairs={{0,4},{4,0},{8,12},{12,8},{16,20},{20,16},{24,28},{28,24},{1,5},{5... | collective-permute-start | bytes 1622024 | tf_op jit(solution)/shard_map/ppermute | solution.py:106
  44.6 21.0 %collective-permute-start.17 = (f16[528,512]{1,0:T(8,128)(2,1)}, f16[528,512]{1,0:T(8,128)(2,1)S(1)}, u32[]{:S(2)}, u32[]{:S(2)}) collective-permute-start(f16[528,512]{1,0:T(8,128)(2,1)} %concatenate.91), channel_id=1, source_target_pairs={{0,4},{4,0},{8,12},{12,8},{16,20},{20,16},{24,28},{28,24},{1,5},{5... | collective-permute-start | bytes 1622024 | tf_op jit(solution)/shard_map/ppermute | solution.py:106
  53.0 32.5 %collective-permute-start.1 = (bf16[2,32,3584]{2,1,0:T(8,128)(2,1)}, bf16[2,32,3584]{2,1,0:T(8,128)(2,1)}, u32[]{:S(2)}, u32[]{:S(2)}) collective-permute-start(bf16[2,32,3584]{2,1,0:T(8,128)(2,1)} %pad_maximum_fusion.5), channel_id=1, source_target_pairs={{0,1},{1,0},{2,3},{3,2},{4,5},{5,4},{6,7},{7,6},{8,9},{9,8},{10,11... | collective-permute-start | bytes 1376264 | tf_op jit(solution)/shard_map/ppermute | solution.py:106
  80.0 76.2 %collective-permute-start.15 = (f16[528,512]{1,0:T(8,128)(2,1)}, f16[528,512]{1,0:T(8,128)(2,1)}, u32[]{:S(2)}, u32[]{:S(2)}) collective-permute-start(f16[528,512]{1,0:T(8,128)(2,1)} %concatenate.89), channel_id=1, source_target_pairs={{0,8},{4,12},{8,0},{12,4},{16,24},{20,28},{24,16},{28,20},{1,9},{5... | collective-permute-start | bytes 1622024 | tf_op jit(solution)/shard_map/ppermute | solution.py:106
  85.0 21.7 %collective-permute-start.18 = (f16[528,512]{1,0:T(8,128)(2,1)}, f16[528,512]{1,0:T(8,128)(2,1)}, u32[]{:S(2)}, u32[]{:S(2)}) collective-permute-start(f16[528,512]{1,0:T(8,128)(2,1)} %concatenate.92), channel_id=1, source_target_pairs={{0,8},{4,12},{8,0},{12,4},{16,24},{20,28},{24,16},{28,20},{1,9},{5... | collective-permute-start | bytes 1622024 | tf_op jit(solution)/shard_map/ppermute | solution.py:106
  101.1 15.9 %collective-permute-start.5 = (f32[4,16,2048]{2,1,0:T(8,128)}, f32[4,16,2048]{2,1,0:T(8,128)}, u32[]{:S(2)}, u32[]{:S(2)}) collective-permute-start(f32[4,16,2048]{2,1,0:T(8,128)} %pad_maximum_fusion.4), channel_id=1, source_target_pairs={{0,8},{4,12},{8,0},{12,4},{16,24},{20,28},{24,16},{28,20},{1,9},{5... | collective-permute-start | bytes 1572872 | tf_op jit(solution)/shard_map/ppermute | solution.py:106
  105.0 14.7 %collective-permute-start.2 = (f32[4,16,2048]{2,1,0:T(8,128)S(1)}, f32[4,16,2048]{2,1,0:T(8,128)S(1)}, u32[]{:S(2)}, u32[]{:S(2)}) collective-permute-start(f32[4,16,2048]{2,1,0:T(8,128)S(1)} %pad_maximum_fusion.3), channel_id=1, source_target_pairs={{0,4},{4,0},{8,12},{12,8},{16,20},{20,16},{24,28},{28,24},{1,5},{5... | collective-permute-start | bytes 1572872 | tf_op jit(solution)/shard_map/ppermute | solution.py:106
  160.1 26.7 %collective-permute-start.19 = (f16[528,512]{1,0:T(8,128)(2,1)}, f16[528,512]{1,0:T(8,128)(2,1)}, u32[]{:S(2)}, u32[]{:S(2)}) collective-permute-start(f16[528,512]{1,0:T(8,128)(2,1)} %concatenate.93), channel_id=1, source_target_pairs={{0,16},{4,20},{8,24},{12,28},{16,0},{20,4},{24,8},{28,12},{1,17},{... | collective-permute-start | bytes 1622024 | tf_op jit(solution)/shard_map/ppermute | solution.py:106
  160.8 27.9 %collective-permute-start.10 = (bf16[4,8,4096]{2,1,0:T(8,128)(2,1)}, bf16[4,8,4096]{2,1,0:T(8,128)(2,1)}, u32[]{:S(2)}, u32[]{:S(2)}) collective-permute-start(bf16[4,8,4096]{2,1,0:T(8,128)(2,1)} %pad_maximum_fusion.8), channel_id=1, source_target_pairs={{0,4},{4,0},{8,12},{12,8},{16,20},{20,16},{24,28},{28,24},{1,5},{5... | collective-permute-start | bytes 786440 | tf_op jit(solution)/shard_map/ppermute | solution.py:106
  215.1 24.6 %collective-permute-start.34 = (f16[528,512]{1,0:T(8,128)(2,1)S(1)}, f16[528,512]{1,0:T(8,128)(2,1)}, u32[]{:S(2)}, u32[]{:S(2)}) collective-permute-start(f16[528,512]{1,0:T(8,128)(2,1)S(1)} %concatenate.100), channel_id=1, source_target_pairs={{0,16},{4,20},{8,24},{12,28},{16,0},{20,4},{24,8},{28,12},{1,17},{... | collective-permute-start | bytes 1622024 | tf_op jit(solution)/shard_map/ppermute | solution.py:106
  215.2 24.5 %collective-permute-start.32 = (f16[528,512]{1,0:T(8,128)(2,1)S(1)}, f16[528,512]{1,0:T(8,128)(2,1)}, u32[]{:S(2)}, u32[]{:S(2)}) collective-permute-start(f16[528,512]{1,0:T(8,128)(2,1)S(1)} %concatenate.100), channel_id=1, source_target_pairs={{0,8},{4,12},{8,0},{12,4},{16,24},{20,28},{24,16},{28,20},{1,9},{5... | collective-permute-start | bytes 1622024 | tf_op jit(solution)/shard_map/ppermute | solution.py:106
  218.0 24.5 %collective-permute-start.21 = (f32[8,8,512]{2,1,0:T(8,128)S(1)}, f32[8,8,512]{2,1,0:T(8,128)S(1)}, u32[]{:S(2)}, u32[]{:S(2)}) collective-permute-start(f32[8,8,512]{2,1,0:T(8,128)S(1)} %add.470), channel_id=1, source_target_pairs={{0,8},{4,12},{8,0},{12,4},{16,24},{20,28},{24,16},{28,20},{1,9},{5... | collective-permute-start | bytes 393224 | tf_op jit(solution)/shard_map/ppermute | solution.py:106
  218.1 28.6 %collective-permute-start.31 = (f16[528,512]{1,0:T(8,128)(2,1)S(1)}, f16[528,512]{1,0:T(8,128)(2,1)}, u32[]{:S(2)}, u32[]{:S(2)}) collective-permute-start(f16[528,512]{1,0:T(8,128)(2,1)S(1)} %concatenate.100), channel_id=1, source_target_pairs={{0,4},{4,0},{8,12},{12,8},{16,20},{20,16},{24,28},{28,24},{1,5},{5... | collective-permute-start | bytes 1622024 | tf_op jit(solution)/shard_map/ppermute | solution.py:106
  239.7 17.5 %collective-permute-start.36 = (f16[528,512]{1,0:T(8,128)(2,1)}, f16[528,512]{1,0:T(8,128)(2,1)}, u32[]{:S(2)}, u32[]{:S(2)}) collective-permute-start(f16[528,512]{1,0:T(8,128)(2,1)} %collective-permute-done.34), channel_id=1, source_target_pairs={{0,8},{4,12},{8,0},{12,4},{16,24},{20,28},{24,16},{28,20},{1,9},{5... | collective-permute-start | bytes 1622024 | tf_op jit(solution)/shard_map/ppermute | solution.py:106
  239.7 19.4 %collective-permute-start.35 = (f16[528,512]{1,0:T(8,128)(2,1)}, f16[528,512]{1,0:T(8,128)(2,1)}, u32[]{:S(2)}, u32[]{:S(2)}) collective-permute-start(f16[528,512]{1,0:T(8,128)(2,1)} %collective-permute-done.34), channel_id=1, source_target_pairs={{0,4},{4,0},{8,12},{12,8},{16,20},{20,16},{24,28},{28,24},{1,5},{5... | collective-permute-start | bytes 1622024 | tf_op jit(solution)/shard_map/ppermute | solution.py:106
  239.7 25.2 %collective-permute-start.33 = (f16[528,512]{1,0:T(8,128)(2,1)}, f16[528,512]{1,0:T(8,128)(2,1)}, u32[]{:S(2)}, u32[]{:S(2)}) collective-permute-start(f16[528,512]{1,0:T(8,128)(2,1)} %collective-permute-done.32), channel_id=1, source_target_pairs={{0,4},{4,0},{8,12},{12,8},{16,20},{20,16},{24,28},{28,24},{1,5},{5... | collective-permute-start | bytes 1622024 | tf_op jit(solution)/shard_map/ppermute | solution.py:106
  242.6 24.3 %collective-permute-start.22 = (f32[8,8,512]{2,1,0:T(8,128)S(1)}, f32[8,8,512]{2,1,0:T(8,128)S(1)}, u32[]{:S(2)}, u32[]{:S(2)}) collective-permute-start(f32[8,8,512]{2,1,0:T(8,128)S(1)} %maximum_add_fusion), channel_id=1, source_target_pairs={{0,16},{4,20},{8,24},{12,28},{16,0},{20,4},{24,8},{28,12},{1,17},{... | collective-permute-start | bytes 393224 | tf_op jit(solution)/shard_map/ppermute | solution.py:106
  266.7 65.1 %collective-permute-start.37 = (f16[528,512]{1,0:T(8,128)(2,1)}, f16[528,512]{1,0:T(8,128)(2,1)S(1)}, u32[]{:S(2)}, u32[]{:S(2)}) collective-permute-start(f16[528,512]{1,0:T(8,128)(2,1)} %collective-permute-done.36), channel_id=1, source_target_pairs={{0,4},{4,0},{8,12},{12,8},{16,20},{20,16},{24,28},{28,24},{1,5},{5... | collective-permute-start | bytes 1622024 | tf_op jit(solution)/shard_map/ppermute | solution.py:106
  280.5 50.5 %collective-permute-start.41 = (f32[8,8,512]{2,1,0:T(8,128)S(1)}, f32[8,8,512]{2,1,0:T(8,128)S(1)}, u32[]{:S(2)}, u32[]{:S(2)}) collective-permute-start(f32[8,8,512]{2,1,0:T(8,128)S(1)} %convolution_bitcast_fusion), channel_id=1, source_target_pairs={{0,1},{1,0},{2,3},{3,2},{4,5},{5,4},{6,7},{7,6},{8,9},{9,8},{10,11... | collective-permute-start | bytes 393224 | tf_op jit(solution)/shard_map/ppermute | solution.py:106
  283.0 71.6 %collective-permute-start.23 = (f32[256,512]{1,0:T(8,128)}, f32[256,512]{1,0:T(8,128)S(1)}, u32[]{:S(2)}, u32[]{:S(2)}) collective-permute-start(f32[256,512]{1,0:T(8,128)} %constant_dynamic-slice_fusion.7), channel_id=1, source_target_pairs={{0,1},{1,0},{2,3},{3,2},{4,5},{5,4},{6,7},{7,6},{8,9},{9,8},{10,11... | collective-permute-start | bytes 1572872 | tf_op jit(solution)/shard_map/ppermute | solution.py:106
  335.6 19.0 %collective-permute-start.43 = (f32[8,8,512]{2,1,0:T(8,128)S(1)}, f32[8,8,512]{2,1,0:T(8,128)S(1)}, u32[]{:S(2)}, u32[]{:S(2)}) collective-permute-start(f32[8,8,512]{2,1,0:T(8,128)S(1)} %add.507), channel_id=1, source_target_pairs={{0,4},{4,0},{8,12},{12,8},{16,20},{20,16},{24,28},{28,24},{1,5},{5... | collective-permute-start | bytes 393224 | tf_op jit(solution)/shard_map/ppermute | solution.py:106
  352.9 26.4 %collective-permute-start.39 = (f32[512,512]{1,0:T(8,128)S(1)}, f32[512,512]{1,0:T(8,128)S(1)}, u32[]{:S(2)}, u32[]{:S(2)}) collective-permute-start(f32[512,512]{1,0:T(8,128)S(1)} %constant_dynamic-slice_fusion.3), channel_id=1, source_target_pairs={{0,1},{1,0},{2,3},{3,2},{4,5},{5,4},{6,7},{7,6},{8,9},{9,8},{10,11... | collective-permute-start | bytes 3145736 | tf_op jit(solution)/shard_map/ppermute | solution.py:106
  372.8 26.1 %collective-permute-start.45 = (f32[8,8,512]{2,1,0:T(8,128)S(1)}, f32[8,8,512]{2,1,0:T(8,128)}, u32[]{:S(2)}, u32[]{:S(2)}) collective-permute-start(f32[8,8,512]{2,1,0:T(8,128)S(1)} %maximum_add_fusion.2), channel_id=1, source_target_pairs={{0,16},{4,20},{8,24},{12,28},{16,0},{20,4},{24,8},{28,12},{1,17},{... | collective-permute-start | bytes 393224 | tf_op jit(solution)/shard_map/ppermute | solution.py:106
  383.2 11.0 %collective-permute-start.29 = (f32[128,512]{1,0:T(8,128)S(1)}, f32[128,512]{1,0:T(8,128)S(1)}, u32[]{:S(2)}, u32[]{:S(2)}) collective-permute-start(f32[128,512]{1,0:T(8,128)S(1)} %maximum_select_fusion.4), channel_id=1, source_target_pairs={{0,2},{1,3},{2,0},{3,1},{4,6},{5,7},{6,4},{7,5},{8,10},{9,11},{10,... | collective-permute-start | bytes 786440 | tf_op jit(solution)/shard_map/ppermute | solution.py:106
  385.5 14.7 %collective-permute-start.40 = (f16[528,512]{1,0:T(8,128)(2,1)S(1)}, f16[528,512]{1,0:T(8,128)(2,1)S(1)}, u32[]{:S(2)}, u32[]{:S(2)}) collective-permute-start(f16[528,512]{1,0:T(8,128)(2,1)S(1)} %concatenate.101), channel_id=1, source_target_pairs={{0,2},{1,3},{2,0},{3,1},{4,6},{5,7},{6,4},{7,5},{8,10},{9,11},{10,... | collective-permute-start | bytes 1622024 | tf_op jit(solution)/shard_map/ppermute | solution.py:106
  386.8 44.5 %collective-permute-start.38 = (f32[512,512]{1,0:T(8,128)S(1)}, f32[512,512]{1,0:T(8,128)S(1)}, u32[]{:S(2)}, u32[]{:S(2)}) collective-permute-start(f32[512,512]{1,0:T(8,128)S(1)} %get-tuple-element.11), channel_id=1, source_target_pairs={{0,1},{1,0},{2,3},{3,2},{4,5},{5,4},{6,7},{7,6},{8,9},{9,8},{10,11... | collective-permute-start | bytes 3145736 | tf_op jit(solution)/shard_map/ppermute | solution.py:106
  441.7 29.3 %collective-permute-start.46 = (f32[1,512,512]{2,1,0:T(8,128)S(1)}, f32[1,512,512]{2,1,0:T(8,128)}, u32[]{:S(2)}, u32[]{:S(2)}) collective-permute-start(f32[1,512,512]{2,1,0:T(8,128)S(1)} %bitcast.194), channel_id=1, source_target_pairs={{0,2},{1,3},{2,0},{3,1},{4,6},{5,7},{6,4},{7,5},{8,10},{9,11},{10,... | collective-permute-start | bytes 3145736 | tf_op jit(solution)/shard_map/ppermute | solution.py:106
  473.8 64.9 %collective-permute-start.47 = (f32[2,512,512]{2,1,0:T(8,128)}, f32[2,512,512]{2,1,0:T(8,128)S(1)}, u32[]{:S(2)}, u32[]{:S(2)}) collective-permute-start(f32[2,512,512]{2,1,0:T(8,128)} %pad_maximum_fusion.1), channel_id=1, source_target_pairs={{0,1},{1,0},{2,3},{3,2},{4,5},{5,4},{6,7},{7,6},{8,9},{9,8},{10,11... | collective-permute-start | bytes 6291464 | tf_op jit(solution)/shard_map/ppermute | solution.py:106
  478.3 30.7 %collective-permute-start.55 = (f32[256,512]{1,0:T(8,128)S(1)}, f32[256,512]{1,0:T(8,128)S(1)}, u32[]{:S(2)}, u32[]{:S(2)}) collective-permute-start(f32[256,512]{1,0:T(8,128)S(1)} %maximum_select_fusion.3), channel_id=1, source_target_pairs={{0,1},{1,0},{2,3},{3,2},{4,5},{5,4},{6,7},{7,6},{8,9},{9,8},{10,11... | collective-permute-start | bytes 1572872 | tf_op jit(solution)/shard_map/ppermute | solution.py:106
  (37 other events, 365.9 us)

commit v2 on v1

v2 whole, which is shorter than its diff:
```python
import math

import jax
import jax.numpy as jnp
from jax import lax
from jax.experimental import pallas as pl
from jax.experimental.pallas import tpu as pltpu
from jax.sharding import PartitionSpec as P

D = 16384
TOK_DEV = 16
HIGH = lax.Precision.HIGH
HIGHEST = lax.Precision.HIGHEST
NN = (((1,), (0,)), ((), ()))
NT = (((1,), (1,)), ((), ()))
TN = (((0,), (0,)), ((), ()))

BLK = 128
TILE = 8


def base_factor(tiles_a, tiles_b, width):
    count = len(tiles_a)
    done_b = [[None] * TILE for _ in range(count)]
    for j in range(0, BLK, width):
        group, first = divmod(j, TILE)
        rows_a = [jnp.broadcast_to(tiles_a[group][first + a : first + a + 1, :], (TILE, BLK)) for a in range(width)]
        rows_b = [jnp.broadcast_to(tiles_b[group][first + a : first + a + 1, :], (TILE, BLK)) for a in range(width)]
        pivot = [[None] * width for _ in range(width)]
        for a in range(width):
            for b in range(a, width):
                pivot[a][b] = jnp.broadcast_to(rows_a[a][:, j + b : j + b + 1], (TILE, BLK))
        inverse = [None] * width
        for a in range(width):
            inverse[a] = 1.0 / pivot[a][a]
            for b in range(a + 1, width):
                factor = pivot[a][b] * inverse[a]
                for c in range(b, width):
                    pivot[b][c] = pivot[b][c] - factor * pivot[a][c]
                rows_a[b] = rows_a[b] - factor * rows_a[a]
                rows_b[b] = rows_b[b] - factor * rows_b[a]
        for a in range(width):
            done_b[group][first + a] = rows_b[a][0:1, :] * lax.rsqrt(pivot[a][a])[0:1, :]
        if j + width >= BLK:
            break
        solved_a, solved_b = [None] * width, [None] * width
        for a in reversed(range(width)):
            left, right = rows_a[a], rows_b[a]
            for b in range(a + 1, width):
                left = left - pivot[a][b] * solved_a[b]
                right = right - pivot[a][b] * solved_b[b]
            solved_a[a], solved_b[a] = left * inverse[a], right * inverse[a]
        for g in range((j + width) // TILE, count):
            left, right = tiles_a[g], tiles_b[g]
            for a in range(width):
                column = jnp.broadcast_to(tiles_a[g][:, j + a : j + a + 1], (TILE, BLK))
                left = left - column * solved_a[a]
                right = right - column * solved_b[a]
            tiles_a[g], tiles_b[g] = left, right
    return [jnp.concatenate(rows, axis=0) for rows in done_b]


def inverse_factor_kernel(gram_ref, out_ref, work, base):
    size = gram_ref.shape[0]
    blocks = size // BLK
    row = lax.broadcasted_iota(jnp.int32, (size, size), 0)
    col = lax.broadcasted_iota(jnp.int32, (size, size), 1)
    work[:, 0:size] = gram_ref[...]
    work[:, size:] = jnp.where(row == col, 1.0, 0.0)
    lane = lax.broadcasted_iota(jnp.int32, (TILE, BLK), 1)
    sub = lax.broadcasted_iota(jnp.int32, (TILE, BLK), 0)
    for k in range(blocks):
        lo, hi = k * BLK, (k + 1) * BLK
        tiles_a = [work[lo + g * TILE : lo + (g + 1) * TILE, lo:hi] for g in range(BLK // TILE)]
        tiles_b = [jnp.where(lane == sub + g * TILE, 1.0, 0.0) for g in range(BLK // TILE)]
        for g, tile in enumerate(base_factor(tiles_a, tiles_b, TILE)):
            base[g * TILE : (g + 1) * TILE, :] = tile
        unit = base[...]
        if k + 1 < blocks:
            right = jnp.dot(unit, work[lo:hi, hi:size], precision=HIGHEST, preferred_element_type=jnp.float32)
        left = jnp.dot(unit, work[lo:hi, size : size + hi], precision=HIGHEST, preferred_element_type=jnp.float32)
        out_ref[lo:hi, 0:hi] = left
        if k + 1 < blocks:
            out_ref[lo:hi, hi:size] = jnp.zeros((BLK, size - hi), jnp.float32)
            tn = (((0,), (0,)), ((), ()))
            work[hi:size, hi:size] -= lax.dot_general(right, right, tn, precision=HIGHEST, preferred_element_type=jnp.float32)
            work[hi:size, size : size + hi] -= lax.dot_general(right, left, tn, precision=HIGHEST, preferred_element_type=jnp.float32)


def inverse_factor(gram):
    size = gram.shape[0]
    return pl.pallas_call(
        inverse_factor_kernel,
        out_shape=jax.ShapeDtypeStruct((size, size), jnp.float32),
        scratch_shapes=[pltpu.VMEM((size, 2 * size), jnp.float32), pltpu.VMEM((BLK, BLK), jnp.float32)],
        compiler_params=pltpu.CompilerParams(vmem_limit_bytes=16 * 1024 * 1024),
        name="inverse_factor",
    )(gram)


def split(x):
    high = x.astype(jnp.bfloat16)
    return high, (x - high.astype(jnp.float32)).astype(jnp.bfloat16)


def mxu(left, right, dims=NN):
    return lax.dot_general(left, right, dims, preferred_element_type=jnp.float32)


def rows_kernel(ids_ref, cov_ref, start_ref, out_ref, top_ref, high, low):
    first = (pl.program_id(0) == 0) & (pl.program_id(1) == 0)

    @pl.when(first)
    def _():
        high[...], low[...] = split(start_ref[...])
        top_ref[...] = jnp.zeros_like(top_ref)

    cov_high, cov_low = split(cov_ref[...])
    image = mxu(cov_high, high[...]) + (mxu(cov_low, high[...]) + mxu(cov_high, low[...]))
    out_ref[0] = image.T
    top_ref[...] = jnp.maximum(top_ref[...], jnp.max(jnp.abs(image), axis=0, keepdims=True))


def rows_times(covariance, start_basis, ids, share):
    width, rank = start_basis.shape
    count = ids.shape[0]
    tall = min(share, 256)
    steps = share // tall
    return pl.pallas_call(
        rows_kernel,
        grid_spec=pltpu.PrefetchScalarGridSpec(
            num_scalar_prefetch=1,
            grid=(count, steps),
            in_specs=[
                pl.BlockSpec((tall, width), lambda p, i, ids_ref: (ids_ref[p] * steps + i, 0)),
                pl.BlockSpec((width, rank), lambda p, i, ids_ref: (0, 0)),
            ],
            out_specs=[
                pl.BlockSpec((1, rank, tall), lambda p, i, ids_ref: (p, 0, i)),
                pl.BlockSpec((8, rank), lambda p, i, ids_ref: (0, 0)),
            ],
            scratch_shapes=[pltpu.VMEM((width, rank), jnp.bfloat16)] * 2,
        ),
        out_shape=[
            jax.ShapeDtypeStruct((count, rank, share), jnp.float32),
            jax.ShapeDtypeStruct((8, rank), jnp.float32),
        ],
        compiler_params=pltpu.CompilerParams(vmem_limit_bytes=40 * 1024 * 1024),
        cost_estimate=pl.CostEstimate(
            flops=6 * count * share * width * rank,
            bytes_accessed=4 * count * share * (width + rank),
            transcendentals=0,
        ),
        name="rows_times",
    )(ids, covariance, start_basis)


def update_kernel(count, rank, per_token, first, ids_ref, cov_ref, row_ref, column_ref, *rest):
    pieces, (out_ref, total_ref, high, low) = rest[:count], rest[-4:]
    p, i = pl.program_id(0), pl.program_id(1)
    kept = row_ref[...]
    steps, _, tall = high.shape

    for k in range(count):

        @pl.when((p == k) & (i == 0))
        def _():
            piece_high, piece_low = split(pieces[k][...])
            for s in range(steps):
                high[s, :rank, :] = piece_high[:, s * tall : (s + 1) * tall]
                low[s] = piece_low[:, s * tall : (s + 1) * tall]

    @pl.when((p == 0) & (i == 0))
    def _():
        total_ref[...] = jnp.zeros_like(total_ref) if first else rest[count][...]

    high[i, rank:, :] = kept
    cov = cov_ref[...]
    out_ref[...] = cov + mxu(kept, column_ref[...], TN) * per_token
    cov_high, cov_low = split(cov)
    total_ref[...] += mxu(high[i], cov_high) + mxu(high[i], cov_low)
    total_ref[:rank, :] += mxu(low[i], cov_high)


def update_and_multiply(covariance, row_data, column_data, pieces, ids, before, updated, per_token):
    count = len(pieces)
    rank, share = pieces[0].shape
    tokens, width = column_data.shape
    tall = min(share, 256)
    steps = share // tall
    high_rows = rank + tokens
    first = before is None

    def fixed(shape):
        return pl.BlockSpec(shape, lambda p, i, ids_ref: (0, 0))

    rows = pl.BlockSpec((tall, width), lambda p, i, ids_ref: (ids_ref[p] * steps + i, 0))
    operands = [covariance, row_data, column_data, *pieces]
    in_specs = [
        rows,
        pl.BlockSpec((tokens, tall), lambda p, i, ids_ref: (0, ids_ref[p] * steps + i)),
        fixed((tokens, width)),
        *[fixed((rank, share))] * count,
    ]
    aliases = {}
    if not first:
        operands += [before, updated]
        in_specs += [fixed((high_rows, width)), pl.BlockSpec(memory_space=pl.ANY)]
        aliases = {len(operands): 0}
    return pl.pallas_call(
        lambda *refs: update_kernel(count, rank, per_token, first, *refs),
        grid_spec=pltpu.PrefetchScalarGridSpec(
            num_scalar_prefetch=1,
            grid=(count, steps),
            in_specs=in_specs,
            out_specs=[rows, fixed((high_rows, width))],
            scratch_shapes=[
                pltpu.VMEM((steps, high_rows, tall), jnp.bfloat16),
                pltpu.VMEM((steps, rank, tall), jnp.bfloat16),
            ],
        ),
        out_shape=[
            jax.ShapeDtypeStruct(covariance.shape, jnp.float32),
            jax.ShapeDtypeStruct((high_rows, width), jnp.float32),
        ],
        input_output_aliases=aliases,
        compiler_params=pltpu.CompilerParams(vmem_limit_bytes=48 * 1024 * 1024),
        cost_estimate=pl.CostEstimate(
            flops=6 * count * share * width * rank,
            bytes_accessed=8 * count * share * width,
            transcendentals=0,
        ),
        name="update_and_multiply",
    )(ids, *operands)


def basis_kernel(scale, ids_ref, factor_ref, image_ref, out_ref):
    factor_high, factor_low = split(factor_ref[...])
    image_high, image_low = split(image_ref[0])
    basis = mxu(factor_high, image_high) + (mxu(factor_high, image_low) + mxu(factor_low, image_high))
    out_ref[...] = basis.T * scale


def basis_of(factor, images, ids, scale):
    count, rank, part = images.shape
    return pl.pallas_call(
        lambda *refs: basis_kernel(scale, *refs),
        grid_spec=pltpu.PrefetchScalarGridSpec(
            num_scalar_prefetch=1,
            grid=(count,),
            in_specs=[
                pl.BlockSpec((rank, rank), lambda p, ids_ref: (0, 0)),
                pl.BlockSpec((1, rank, part), lambda p, ids_ref: (ids_ref[p], 0, 0)),
            ],
            out_specs=pl.BlockSpec((part, rank), lambda p, ids_ref: (p, 0)),
        ),
        out_shape=jax.ShapeDtypeStruct((count * part, rank), jnp.float32),
        compiler_params=pltpu.CompilerParams(vmem_limit_bytes=32 * 1024 * 1024),
        cost_estimate=pl.CostEstimate(
            flops=6 * count * part * rank * rank, bytes_accessed=8 * count * part * rank, transcendentals=0
        ),
        name="basis_of",
    )(ids, factor, images)


def dot(left, right, dims=NN, precision=HIGH):
    return lax.dot_general(left, right, dims, precision=precision, preferred_element_type=jnp.float32)


def swap(x, axis, bit):
    return lax.ppermute(x, axis, [(i, i ^ bit) for i in range(lax.axis_size(axis))])


def bits_of(axis):
    return [1 << b for b in range(lax.axis_size(axis).bit_length() - 1)]


def power_over(top):
    exponent = jnp.where(top > 0, jnp.ceil(jnp.log2(top)), 0.0)
    return jnp.full((8, 128), jnp.maximum(exponent, -90.0), jnp.float32)


def pack(x, power):
    return (x * jnp.exp2(15.0 - power[0, 0])).astype(jnp.float16)


def unpack(message, power):
    return message.astype(jnp.float32) * jnp.exp2(power[0, 0] - 15.0)


def block(x, index, size, axis):
    return lax.dynamic_slice_in_dim(x, index * size, size, axis)


def gather_relative(x, axis, bits):
    held = {0: x}
    for bit in bits:
        for m in sorted(held):
            held[m ^ bit] = swap(held[m], axis, bit)
    return held


def gather_rows(x, axis, bits):
    for bit in bits:
        x = jnp.concatenate([x, swap(x, axis, bit)], axis=0)
    return x


def mirror(m, axis):
    bits = bits_of(axis)
    return sum(((m // bit) & 1) * other for bit, other in zip(bits, bits[::-1]))


def sum_whole(x, axes):
    for axis in axes:
        for bit in bits_of(axis)[::-1]:
            x = x + swap(x, axis, bit)
    return x


def side_of(axis, bit):
    return (lax.axis_index(axis) & bit) // bit


def sum_halves(x, axis):
    for bit in bits_of(axis):
        half, side = x.shape[0] // 2, side_of(axis, bit)
        x = block(x, side, half, 0) + swap(block(x, 1 - side, half, 0), axis, bit)
    return x


def join_halves(x, axis):
    for bit in bits_of(axis)[::-1]:
        other = swap(x, axis, bit)
        x = jnp.where(side_of(axis, bit) == 0, jnp.concatenate([x, other]), jnp.concatenate([other, x]))
    return x


def tie(*values):
    return lax.optimization_barrier(values)


def scatter_step(held, bit):
    leaving = [m for m in sorted(held) if m & bit]
    return jnp.stack([held.pop(m) for m in leaving]), leaving


def scatter_add(held, came, leaving, bit):
    for at, m in enumerate(leaving):
        held[m ^ bit] = held[m ^ bit] + came[at]


def body(hidden, down_weight, covariance, keep_index, start_basis):
    f_count, t_count = lax.axis_size("fsdp"), lax.axis_size("tensor")
    f, t = lax.axis_index("fsdp"), lax.axis_index("tensor")
    f_bits, t_bits = bits_of("fsdp"), bits_of("tensor")
    quarter, width = covariance.shape
    rank = start_basis.shape[1]
    share = quarter // f_count
    group = f_count // t_count
    part = width // t_count
    root = math.sqrt(D)
    per_token = 1.0 / (TOK_DEV * f_count)

    tokens = gather_rows(hidden, "tensor", t_bits[::-1])
    leaving = sorted((m for m in range(f_count) if m & 1), key=lambda m: (-(m & 2), -m))
    staying = sorted((m for m in range(f_count) if not m & 1), reverse=True)
    sent, top_sent = rows_times(covariance, start_basis, f ^ jnp.array(leaving, jnp.int32), share)
    power_sent = power_over(jnp.max(top_sent))
    power_came = swap(power_sent, "fsdp", 1)
    per_message = len(leaving) // 2
    tokens, power_came, message, message_later = tie(
        tokens, power_came, pack(sent[:per_message], power_sent), pack(sent[per_message:], power_sent)
    )

    partial_out = jnp.dot(tokens, down_weight, preferred_element_type=jnp.float32)
    came_early = swap(message, "fsdp", 1)
    came_early, partial_out, message_later = tie(came_early, partial_out, message_later)

    def token_rows(x, m):
        owner = f ^ m
        place = mirror((owner // group) ^ t, "tensor")
        return block(x, place * group + owner % group, TOK_DEV, 0)

    half = partial_out.shape[1] // 2
    orders = (f_bits[1:] + f_bits[:1], f_bits[:0:-1] + f_bits[:1])
    token_sums = [{m: token_rows(partial_out[:, at : at + half], m) for m in range(f_count)} for at in (0, half)]

    def token_step(step):
        return [scatter_step(held, order[step]) for held, order in zip(token_sums, orders)]

    def token_add(step, left, came):
        for held, order, (_, gone), arrived in zip(token_sums, orders, left, came):
            scatter_add(held, arrived, gone, order[step])

    def token_swap(step, messages):
        return [swap(message, "fsdp", order[step]) for message, order in zip(messages, orders)]

    left = token_step(0)
    start_later, message_later, *messages = tie(start_basis, message_later, *[message for message, _ in left])

    came_late = swap(message_later, "fsdp", 1)
    came = token_swap(0, messages)
    stayed, top_stayed = rows_times(covariance, start_later, f ^ jnp.array(staying, jnp.int32), share)
    came_late, stayed, top_stayed, *came = tie(came_late, stayed, top_stayed, *came)
    token_add(0, left, came)
    power = jnp.maximum(power_over(jnp.maximum(jnp.max(top_sent), jnp.max(top_stayed))), power_came)
    powers = []
    for bit in f_bits[1:]:
        power = jnp.maximum(power, swap(power, "fsdp", bit))
        powers.append(power + (len(powers) + 1))
    held = {m: stayed[i] for i, m in enumerate(staying)}
    scatter_add(held, unpack(came_early, power_came), leaving[:per_message], 1)
    scatter_add(held, unpack(came_late, power_came), leaving[per_message:], 1)

    power, *powers = tie(power, *powers)
    for step in range(1, len(f_bits)):
        image, gone = scatter_step(held, f_bits[step])
        left = token_step(step)
        image, *messages = tie(pack(image, powers[step - 1]), *[message for message, _ in left])
        came = token_swap(step, messages)
        image_came = swap(image, "fsdp", f_bits[step])
        if step == 1:
            power_other = swap(power, "fsdp", 1)
            image_came, power_other, *came = tie(image_came, power_other, *came)
            power = jnp.maximum(power, power_other) + len(f_bits)
        elif step + 1 < len(f_bits):
            image_came, *came = tie(image_came, *came)
        token_add(step, left, came)
        if step + 1 < len(f_bits):
            scatter_add(held, unpack(image_came, powers[step - 1]), gone, f_bits[step])
    mlp_out = jnp.concatenate([held_rows[0] for held_rows in token_sums], axis=1).astype(jnp.bfloat16)

    positions = jnp.arange(TOK_DEV, dtype=jnp.int32)
    picks = (keep_index[0][:, None] == positions[None, :]).astype(jnp.bfloat16)
    row_data = jnp.dot(picks, mlp_out, preferred_element_type=jnp.float32).astype(jnp.bfloat16)
    slots = row_data.shape[0]
    order = jnp.arange(f_count * slots, dtype=jnp.int32)
    source = mirror((order // slots) ^ f, "fsdp") * slots + order % slots
    arrange = (source[:, None] == order[None, :]).astype(jnp.bfloat16)
    row_data = gather_rows(row_data, "fsdp", f_bits[:1:-1])
    row_data, image_came = tie(row_data, image_came)
    scatter_add(held, unpack(image_came, powers[-1]), gone, f_bits[-1])
    raw = held[0]

    pieces = {0: pack(raw, power)}

    def gather_stage(weight):
        chosen = [m for m in range(f_count) if m.bit_count() == weight]
        return {m: swap(pieces[m & (m - 1)], "fsdp", m & -m) for m in chosen}

    def settle(stage, *others):
        done = tie(*stage.values(), *others)
        pieces.update(zip(stage, done))
        return done[len(stage) :]

    row_data, pieces[0] = tie(gather_rows(row_data, "fsdp", f_bits[1:2]), pieces[0])
    stage = gather_stage(1)
    row_data = gather_rows(row_data, "fsdp", f_bits[:1])
    row_data = jnp.dot(arrange, row_data, preferred_element_type=jnp.float32).astype(jnp.bfloat16)
    gram_part = sum_halves(dot(raw, raw, NT, HIGHEST), "tensor")
    row_data, gram_part = settle(stage, row_data, gram_part)
    own_rows = block(row_data, f, share, 1).astype(jnp.float32)
    for weight in range(2, len(f_bits)):
        stage = gather_stage(weight)
        if weight == 2:
            column_data = block(row_data, f % group, width, 1) * (t == f // group).astype(jnp.bfloat16)
            column_data = sum_whole(column_data, ["tensor"])
            both = jnp.concatenate([raw, own_rows], axis=0)
            products = sum_whole(dot(own_rows, both, NT), ["tensor"])
            kept_start = dot(column_data.astype(jnp.float32), start_basis)
            column_data, products, kept_start = settle(stage, column_data, products, kept_start)
        else:
            settle(stage)

    def small_step(bit, values):
        return [swap(value, "fsdp", bit) for value in values]

    small = [kept_start, products, gram_part]
    for bit in f_bits[:2:-1]:
        small = [a + b for a, b in zip(small, tie(*small_step(bit, small)))]
    stage = gather_stage(len(f_bits))
    came = small_step(f_bits[2], small)
    total = new_covariance = None
    for odd in (0, 1):
        chosen = [m for m in range(f_count) if m & 1 == odd]
        new_covariance, total = update_and_multiply(
            covariance,
            row_data,
            column_data,
            [raw if m == 0 else unpack(pieces[m], power) for m in chosen],
            f ^ jnp.array(chosen, jnp.int32),
            total,
            new_covariance,
            per_token,
        )
        if odd == 0:
            total, new_covariance, *came = settle(stage, total, new_covariance, *came)
            small = [a + b for a, b in zip(small, came)]
            came = small_step(f_bits[1], small)
        else:
            total, new_covariance, *came = tie(total, new_covariance, *came)
            small = [a + b for a, b in zip(small, came)]
    seconds = {m: block(total, t ^ m, part, 1) for m in range(t_count)}
    came = small_step(1, small)
    for at, bit in enumerate(t_bits):
        leave, gone = scatter_step(seconds, bit)
        if at == 0:
            arrived = swap(leave, "tensor", bit)
            arrived, *came = tie(arrived, *came)
            kept_start, products, gram_part = [a + b for a, b in zip(small, came)]
            kept_start = kept_start * per_token
            raw_gram = join_halves(gram_part, "tensor")
            kept_raw, kept_square = products[:, :rank], products[:, rank:]
            kept_image = kept_raw + dot(kept_square, kept_start)
            middle = dot(kept_start, (kept_raw + kept_image) * 0.5, TN)
            first_gram = raw_gram + middle + middle.T
        else:
            images, kept = leave[:, :rank], leave[:, rank:]
            power_left = power_over(jnp.max(jnp.abs(images)))
            power_other = swap(power_left, "tensor", bit)
            message, power_other, kept, first_gram = tie(pack(images, power_left), power_other, kept, first_gram)
            arrived = [swap(message, "tensor", bit), swap(kept, "tensor", bit)]
            if at == 1:
                first_inverse = inverse_factor(first_gram)
                *arrived, first_inverse = tie(*arrived, first_inverse)
            arrived = jnp.concatenate([unpack(arrived[0], power_other), arrived[1]], axis=1)
        scatter_add(seconds, arrived, gone, bit)
    second = (
        seconds[0][:rank]
        + dot(kept_start, seconds[0][rank:], TN)
        + dot(kept_image, block(column_data, t, part, 1).astype(jnp.float32) * per_token, TN)
    )

    second = dot(first_inverse, second)
    second, last_gram = tie(second, sum_halves(dot(second, second, NT, HIGHEST), "tensor"))
    arrived = swap(second, "tensor", t_bits[-1])
    for bit in f_bits[::-1]:
        last_gram = last_gram + swap(last_gram, "fsdp", bit)
    arrived, last_gram = tie(arrived, last_gram)
    last_gram = join_halves(last_gram, "tensor")
    parts = gather_rows(jnp.stack([second, arrived]), "tensor", t_bits[-2::-1])
    own = raw + dot(kept_start, own_rows, TN)
    first_basis = lax.dot_general(
        own, first_inverse, (((0,), (1,)), ((), ())), precision=HIGH, preferred_element_type=jnp.float32
    ) * root
    last_gram, parts, first_basis = tie(last_gram, parts, first_basis)
    last_inverse = inverse_factor(last_gram)
    places = jnp.stack([mirror(t ^ m, "tensor") for m in range(t_count)])
    final_basis = basis_of(last_inverse, parts, places, root)
    return (mlp_out, new_covariance, first_basis, final_basis)


def solution(mesh):
    placed = (
        P("tensor", "fsdp"),
        P("fsdp", "tensor"),
        P("tensor", "fsdp"),
        P("fsdp", None),
        P("fsdp", None),
    )
    return jax.shard_map(
        body,
        mesh=mesh,
        in_specs=placed,
        out_specs=(
            P("fsdp", "tensor"),
            P("tensor", "fsdp"),
            P(("tensor", "fsdp"), None),
            P("fsdp", None),
        ),
        check_vma=False,
    )
```

time: 557 us -> 464 us (0.83)
  matrix products: 192 us -> 25 us
  Pallas kernels: 59.2 us -> 146 us
  local copies, waits for them, and re-layouts: 39 us -> 19.6 us
  between operations: 25.2 us -> 11.8 us
  waiting for transfers between devices: 132 us -> 145 us
  other arithmetic: 33.1 us -> 44.4 us
    dot_general x31 -> x10, matrix products: 151 us -> 8.98 us  [dot(): lax.dot_general(left, right, dims, precision=precision, preferred_element...]
    pallas_call x0 -> x5, Pallas kernels: none -> 95.2 us  [the longest x2 51.2 us: update_and_multiply(): pl.pallas_call(lambda *refs: update_kernel(count, rank, per_token, first,...]
    dot_general x1, matrix products: 25 us -> 1.28 us  [body(): jnp.dot(arrange, row_data, preferred_element_type=jnp.float32)]
    slice x22 -> x7, local copies, waits for them, and re-layouts: 18.5 us -> 4.35 us  [the longest x3 1.6 us: pack(): return (x * jnp.exp2(15.0 - power[0, 0])).astype(jnp.float16)]
    ppermute x56, waiting for transfers between devices: 132 us -> 145 us  [swap(): lax.ppermute(x, axis, [(i, i ^ bit) for i in range(lax.axis_size(axis))])]
    pallas_call x2, Pallas kernels: 59.2 us -> 51 us  [inverse_factor(): pl.pallas_call(inverse_factor_kernel, out_shape=jax.ShapeDtypeStruct((siz...]
    concatenate x9 -> x0, local copies, waits for them, and re-layouts: 6.77 us -> none  [pack(): jnp.concatenate([values, jnp.full((PAD, x.shape[1]), power, jnp.float16)]...]
    add x17 -> x26, other arithmetic: 1.59 us -> 7.53 us  [the longest x2 4.12 us: scatter_add(): held[m ^ bit] = held[m ^ bit] + came[at]]
  transfers between devices with their start and end apart: 56 -> 56, of which waited for: 24 -> 19; matrix products, arithmetic and copies ran while one was open for 43% -> 10% of each run, Pallas kernels for 11% -> 25%
where the time goes in v2:
time: 464 us; the launch traced here: 457 us
  Pallas kernels  146 us (31%)
  waiting for transfers between devices  145 us (31%)
  starting transfers between devices  65 us (14%)
  other arithmetic  44.4 us (10%)
  matrix products  25 us (5%)
  local copies, waits for them, and re-layouts  19.6 us (4%)
  between operations  11.8 us (3%)
    ppermute x56, waiting for transfers between devices, swap(): lax.ppermute(x, axis, [(i, i ^ bit) for i in range(lax.axis_size(axis))])  145 us
    ppermute x56, starting transfers between devices, swap(): lax.ppermute(x, axis, [(i, i ^ bit) for i in range(lax.axis_size(axis))])  65 us
    pallas_call x2, Pallas kernels, update_and_multiply(): pl.pallas_call(lambda *refs: update_kernel(count, rank, per_token, first,...  51.2 us
    pallas_call x2, Pallas kernels, inverse_factor(): pl.pallas_call(inverse_factor_kernel, out_shape=jax.ShapeDtypeStruct((siz...  51 us
    pallas_call x2, Pallas kernels, rows_times(): pl.pallas_call(rows_kernel, grid_spec=pltpu.PrefetchScalarGridSpec(num_sc...  37.6 us
    unnamed x54, local copies, waits for them, and re-layouts  11.9 us
    dot_general x1, matrix products, body(): jnp.dot(tokens, down_weight, preferred_element_type=jnp.float32)  11.7 us
    convert_element_type x5, other arithmetic, pack(): return (x * jnp.exp2(15.0 - power[0, 0])).astype(jnp.float16)  10.7 us
  transfers between devices with their start and end apart: 56, of which 19 were waited for; matrix products, arithmetic and copies ran while one was open for 10% of the time, Pallas kernels for 25%

profile of v2, /device:TPU:1, one launch (start us, length us, event | category | flops | bytes accessed | tf_op | source)
XLA Modules:
  0.0 457.5 jit_solution(7912281082190439622)
XLA Ops:
  3.4 4.9 %collective-permute-done = bf16[32,3584]{1,0:T(8,128)(2,1)S(1)} collective-permute-done((bf16[32,3584]{1,0:T(8,128)(2,1)}, bf16[32,3584]{1,0:T(8,128)(2,1)S(1)}, u32[]{:S(2)}, u32[]{:S(2)}) %collective-permute-start) | collective-permute-done | bytes 229408 | tf_op jit(solution)/shard_map/ppermute | solution.py:271
  12.8 18.8 %rows_times.2 = (f32[4,512,512]{2,1,0:T(8,128)S(1)}, f32[8,512]{1,0:T(8,128)S(1)}) custom-call(s32[4]{0:T(128)S(1)} %get-tuple-element.195.ids_ref, f32[4096,2048]{1,0:T(8,128)} %refs_1_.3, f32[2048,512]{1,0:T(8,128)S(1)} %copy-done.2), custom_call_target="tpu_custom_call" | custom-call | flops 12884901888 | bytes 20971520 | tf_op jit(solution)/shard_map/rows_times/pallas_call | solution.py:129
  37.1 2.9 multiply_convert_fusion
  41.7 11.7 %fusion.50 = f32[128,4096]{1,0:T(8,128)S(1)} fusion(bf16[128,3584]{1,0:T(8,128)(2,1)S(1)} %pad_maximum_fusion.3, bf16[3584,4096]{1,0:T(8,128)(2,1)} %param.10), kind=kOutput, calls=%fused_computation.156 | convolution fusion | flops 3758096384 | bytes 32374784 | tf_op jit(solution)/shard_map/dot_general | solution.py:376
  53.4 11.2 %collective-permute-done.3 = f16[2,512,512]{2,1,0:T(8,128)(2,1)S(1)} collective-permute-done((f16[2,512,512]{2,1,0:T(8,128)(2,1)S(1)}, f16[2,512,512]{2,1,0:T(8,128)(2,1)S(1)}, u32[]{:S(2)}, u32[]{:S(2)}) %collective-permute-start.3) | collective-permute-done | bytes 1048608 | tf_op jit(solution)/shard_map/ppermute | solution.py:271
  69.8 18.9 %rows_times.3 = (f32[4,512,512]{2,1,0:T(8,128)S(1)}, f32[8,512]{1,0:T(8,128)S(1)}) custom-call(s32[4]{0:T(128)S(1)} %get-tuple-element.194.ids_ref, f32[4096,2048]{1,0:T(8,128)} %refs_1_.3, f32[2048,512]{1,0:T(8,128)S(1)} %copy-done.3), custom_call_target="tpu_custom_call" | custom-call | flops 12884901888 | bytes 20971520 | tf_op jit(solution)/shard_map/rows_times/pallas_call | solution.py:129
  111.3 19.5 %collective-permute-done.11 = f32[2,16,2048]{2,1,0:T(8,128)S(1)} collective-permute-done((f32[2,16,2048]{2,1,0:T(8,128)}, f32[2,16,2048]{2,1,0:T(8,128)S(1)}, u32[]{:S(2)}, u32[]{:S(2)}) %collective-permute-start.11) | collective-permute-done | bytes 262176 | tf_op jit(solution)/shard_map/ppermute | solution.py:271
  130.7 9.9 %collective-permute-done.12 = f32[2,16,2048]{2,1,0:T(8,128)S(1)} collective-permute-done((f32[2,16,2048]{2,1,0:T(8,128)}, f32[2,16,2048]{2,1,0:T(8,128)S(1)}, u32[]{:S(2)}, u32[]{:S(2)}) %collective-permute-start.12) | collective-permute-done | bytes 262176 | tf_op jit(solution)/shard_map/ppermute | solution.py:271
  155.8 21.6 %collective-permute-done.15 = bf16[8,4096]{1,0:T(8,128)(2,1)S(1)} collective-permute-done((bf16[8,4096]{1,0:T(8,128)(2,1)S(1)}, bf16[8,4096]{1,0:T(8,128)(2,1)S(1)}, u32[]{:S(2)}, u32[]{:S(2)}) %collective-permute-start.15) | collective-permute-done | bytes 65568 | tf_op jit(solution)/shard_map/ppermute | solution.py:271
  177.4 2.8 multiply_convert_fusion.3
  182.7 5.2 %collective-permute-done.17 = bf16[16,4096]{1,0:T(8,128)(2,1)} collective-permute-done((bf16[16,4096]{1,0:T(8,128)(2,1)S(1)}, bf16[16,4096]{1,0:T(8,128)(2,1)}, u32[]{:S(2)}, u32[]{:S(2)}) %collective-permute-start.17) | collective-permute-done | bytes 131104 | tf_op jit(solution)/shard_map/ppermute | solution.py:271
  193.8 13.6 %collective-permute-done.21 = bf16[32,4096]{1,0:T(8,128)(2,1)} collective-permute-done((bf16[32,4096]{1,0:T(8,128)(2,1)S(1)}, bf16[32,4096]{1,0:T(8,128)(2,1)}, u32[]{:S(2)}, u32[]{:S(2)}) %collective-permute-start.21) | collective-permute-done | bytes 262176 | tf_op jit(solution)/shard_map/ppermute | solution.py:271
  208.7 3.8 collective-permute-done.19
  219.8 4.6 %collective-permute-start.30 = (f32[64,576]{1,0:T(8,128)S(1)}, f32[64,576]{1,0:T(8,128)S(1)}, u32[]{:S(2)}, u32[]{:S(2)}) collective-permute-start(f32[64,576]{1,0:T(8,128)S(1)} %add.526), channel_id=1, source_target_pairs={{0,1},{1,0},{2,3},{3,2},{4,5},{5,4},{6,7},{7,6},{8,9},{9,8},{10,11... | collective-permute-start | bytes 442376 | tf_op jit(solution)/shard_map/ppermute | solution.py:271
  224.5 2.8 collective-permute-start.28
  230.9 2.4 collective-permute-done.24
  234.1 4.5 collective-permute-start.33
  238.7 25.1 %update_and_multiply.2 = (f32[4096,2048]{1,0:T(8,128)}, f32[576,2048]{1,0:T(8,128)}) custom-call(s32[4]{0:T(128)S(1)} %get-tuple-element.192.refs_0_, f32[4096,2048]{1,0:T(8,128)} %refs_1_.3, bf16[64,4096]{1,0:T(8,128)(2,1)S(1)} %convolution_convert_fusion.refs_2_, bf16[64,2048]{1,0:T(8,128)(2,1)S(1)} %add.524.refs_3_, ...), custom_call_target="tpu_custom_call" | custom-call | flops 12884901888 | bytes 33554432 | tf_op jit(solution)/shard_map/update_and_multiply/pallas_call | solution.py:210
  267.1 26.1 %update_and_multiply.3 = (f32[4096,2048]{1,0:T(8,128)}, f32[576,2048]{1,0:T(8,128)}) custom-call(s32[4]{0:T(128)S(1)} %get-tuple-element.193.refs_0_, f32[4096,2048]{1,0:T(8,128)} %refs_1_.3, bf16[64,4096]{1,0:T(8,128)(2,1)S(1)} %convolution_convert_fusion.refs_2_, bf16[64,2048]{1,0:T(8,128)(2,1)S(1)} %add.524.refs_3_, ...), custom_call_target="tpu_custom_call", output_to_operand_aliasing={{0}: (9, {})} | custom-call | flops 12884901888 | bytes 33554432 | tf_op jit(solution)/shard_map/update_and_multiply/pallas_call | solution.py:210
  296.8 4.8 %collective-permute-start.38 = (f32[2,576,512]{2,1,0:T(8,128)}, f32[2,576,512]{2,1,0:T(8,128)}, u32[]{:S(2)}, u32[]{:S(2)}) collective-permute-start(f32[2,576,512]{2,1,0:T(8,128)} %pad_maximum_fusion.1), channel_id=1, source_target_pairs={{0,1},{1,0},{2,3},{3,2},{4,5},{5,4},{6,7},{7,6},{8,9},{9,8},{10,11... | collective-permute-start | bytes 7077896 | tf_op jit(solution)/shard_map/ppermute | solution.py:271
  304.0 11.9 %collective-permute-done.39 = f32[64,512]{1,0:T(8,128)S(1)} collective-permute-done((f32[64,512]{1,0:T(8,128)S(1)}, f32[64,512]{1,0:T(8,128)S(1)}, u32[]{:S(2)}, u32[]{:S(2)}) %collective-permute-start.39) | collective-permute-done | bytes 131104 | tf_op jit(solution)/shard_map/ppermute | solution.py:271
  330.4 2.6 fusion.12.gram_ref
  335.7 25.4 %inverse_factor.2 = f32[512,512]{1,0:T(8,128)S(1)} custom-call(f32[512,512]{1,0:T(8,128)S(1)} %copy-done), custom_call_target="tpu_custom_call" | custom-call | tf_op jit(solution)/shard_map/inverse_factor/pallas_call | solution.py:92
  372.8 6.5 %collective-permute-done.48 = f32[128,512]{1,0:T(8,128)S(1)} collective-permute-done((f32[128,512]{1,0:T(8,128)S(1)}, f32[128,512]{1,0:T(8,128)S(1)}, u32[]{:S(2)}, u32[]{:S(2)}) %collective-permute-start.48) | collective-permute-done | bytes 262176 | tf_op jit(solution)/shard_map/ppermute | solution.py:271
  382.0 11.7 %collective-permute-done.50 = f32[128,512]{1,0:T(8,128)S(1)} collective-permute-done((f32[128,512]{1,0:T(8,128)S(1)}, f32[128,512]{1,0:T(8,128)S(1)}, u32[]{:S(2)}, u32[]{:S(2)}) %collective-permute-start.50) | collective-permute-done | bytes 262176 | tf_op jit(solution)/shard_map/ppermute | solution.py:271
  394.0 5.5 %collective-permute-done.51 = f32[128,512]{1,0:T(8,128)S(1)} collective-permute-done((f32[128,512]{1,0:T(8,128)S(1)}, f32[128,512]{1,0:T(8,128)S(1)}, u32[]{:S(2)}, u32[]{:S(2)}) %collective-permute-start.51) | collective-permute-done | bytes 262176 | tf_op jit(solution)/shard_map/ppermute | solution.py:271
  400.4 4.5 collective-permute-done.52
  406.6 4.1 collective-permute-start.55
  411.2 7.4 %collective-permute-done.53 = f32[128,512]{1,0:T(8,128)S(1)} collective-permute-done((f32[128,512]{1,0:T(8,128)S(1)}, f32[128,512]{1,0:T(8,128)S(1)}, u32[]{:S(2)}, u32[]{:S(2)}) %collective-permute-start.53) | collective-permute-done | bytes 262176 | tf_op jit(solution)/shard_map/ppermute | solution.py:271
  420.0 2.8 convolution_multiply_fusion
  425.0 25.5 %inverse_factor.3.refs_1_ = f32[512,512]{1,0:T(8,128)S(1)} custom-call(f32[512,512]{1,0:T(8,128)S(1)} %maximum_select_fusion.1.gram_ref), custom_call_target="tpu_custom_call" | custom-call | tf_op jit(solution)/shard_map/inverse_factor/pallas_call | solution.py:92
  450.6 6.4 %basis_of.1 = f32[2048,512]{1,0:T(8,128)} custom-call(s32[4]{0:T(128)S(1)} %pad_add_fusion.refs_0_, f32[512,512]{1,0:T(8,128)S(1)} %inverse_factor.3.refs_1_, f32[4,512,512]{2,1,0:T(8,128)S(1)} %pad_maximum_fusion.refs_2_), custom_call_target="tpu_custom_call" | custom-call | flops 3221225472 | bytes 8388608 | tf_op jit(solution)/shard_map/basis_of/pallas_call | solution.py:246
  (246 shorter events, 116.6 us)
Async XLA Ops:
  9.3 30.6 %collective-permute-start.1 = (bf16[64,3584]{1,0:T(8,128)(2,1)S(1)}, bf16[64,3584]{1,0:T(8,128)(2,1)S(1)}, u32[]{:S(2)}, u32[]{:S(2)}) collective-permute-start(bf16[64,3584]{1,0:T(8,128)(2,1)S(1)} %pad_maximum_fusion.6), channel_id=1, source_target_pairs={{0,1},{1,0},{2,3},{3,2},{4,5},{5,4},{6,7},{7,6},{8,9},{9,8},{10,11... | collective-permute-start | bytes 1376264 | tf_op jit(solution)/shard_map/ppermute | solution.py:271
  40.0 24.5 %collective-permute-start.3 = (f16[2,512,512]{2,1,0:T(8,128)(2,1)S(1)}, f16[2,512,512]{2,1,0:T(8,128)(2,1)S(1)}, u32[]{:S(2)}, u32[]{:S(2)}) collective-permute-start(f16[2,512,512]{2,1,0:T(8,128)(2,1)S(1)} %get-tuple-element.87), channel_id=1, source_target_pairs={{0,4},{4,0},{8,12},{12,8},{16,20},{20,16},{24,28},{28,24},{1,5},{5... | collective-permute-start | bytes 3145736 | tf_op jit(solution)/shard_map/ppermute | solution.py:271
  65.7 25.3 %collective-permute-start.4 = (f16[2,512,512]{2,1,0:T(8,128)(2,1)S(1)}, f16[2,512,512]{2,1,0:T(8,128)(2,1)S(1)}, u32[]{:S(2)}, u32[]{:S(2)}) collective-permute-start(f16[2,512,512]{2,1,0:T(8,128)(2,1)S(1)} %get-tuple-element.92), channel_id=1, source_target_pairs={{0,4},{4,0},{8,12},{12,8},{16,20},{20,16},{24,28},{28,24},{1,5},{5... | collective-permute-start | bytes 3145736 | tf_op jit(solution)/shard_map/ppermute | solution.py:271
  66.2 24.8 %collective-permute-start.5 = (f32[4,16,2048]{2,1,0:T(8,128)S(1)}, f32[4,16,2048]{2,1,0:T(8,128)S(1)}, u32[]{:S(2)}, u32[]{:S(2)}) collective-permute-start(f32[4,16,2048]{2,1,0:T(8,128)S(1)} %pad_maximum_fusion.4), channel_id=1, source_target_pairs={{0,8},{4,12},{8,0},{12,4},{16,24},{20,28},{24,16},{28,20},{1,9},{5... | collective-permute-start | bytes 1572872 | tf_op jit(solution)/shard_map/ppermute | solution.py:271
  67.5 23.5 %collective-permute-start.6 = (f32[4,16,2048]{2,1,0:T(8,128)S(1)}, f32[4,16,2048]{2,1,0:T(8,128)S(1)}, u32[]{:S(2)}, u32[]{:S(2)}) collective-permute-start(f32[4,16,2048]{2,1,0:T(8,128)S(1)} %pad_maximum_fusion.5), channel_id=1, source_target_pairs={{0,16},{4,20},{8,24},{12,28},{16,0},{20,4},{24,8},{28,12},{1,17},{... | collective-permute-start | bytes 1572872 | tf_op jit(solution)/shard_map/ppermute | solution.py:271
  105.9 34.8 %collective-permute-start.9 = (f16[2,512,512]{2,1,0:T(8,128)(2,1)}, f16[2,512,512]{2,1,0:T(8,128)(2,1)}, u32[]{:S(2)}, u32[]{:S(2)}) collective-permute-start(f16[2,512,512]{2,1,0:T(8,128)(2,1)} %fusion), channel_id=1, source_target_pairs={{0,8},{4,12},{8,0},{12,4},{16,24},{20,28},{24,16},{28,20},{1,9},{5... | collective-permute-start | bytes 3145736 | tf_op jit(solution)/shard_map/ppermute | solution.py:271
  106.6 24.1 %collective-permute-start.11 = (f32[2,16,2048]{2,1,0:T(8,128)}, f32[2,16,2048]{2,1,0:T(8,128)S(1)}, u32[]{:S(2)}, u32[]{:S(2)}) collective-permute-start(f32[2,16,2048]{2,1,0:T(8,128)} %pad_maximum_fusion.7), channel_id=1, source_target_pairs={{0,16},{4,20},{8,24},{12,28},{16,0},{20,4},{24,8},{28,12},{1,17},{... | collective-permute-start | bytes 786440 | tf_op jit(solution)/shard_map/ppermute | solution.py:271
  107.2 33.5 %collective-permute-start.12 = (f32[2,16,2048]{2,1,0:T(8,128)}, f32[2,16,2048]{2,1,0:T(8,128)S(1)}, u32[]{:S(2)}, u32[]{:S(2)}) collective-permute-start(f32[2,16,2048]{2,1,0:T(8,128)} %pad_maximum_fusion.8), channel_id=1, source_target_pairs={{0,8},{4,12},{8,0},{12,4},{16,24},{20,28},{24,16},{28,20},{1,9},{5... | collective-permute-start | bytes 786440 | tf_op jit(solution)/shard_map/ppermute | solution.py:271
  149.5 27.9 %collective-permute-start.16 = (f16[1,512,512]{2,1,0:T(8,128)(2,1)S(1)}, f16[1,512,512]{2,1,0:T(8,128)(2,1)S(1)}, u32[]{:S(2)}, u32[]{:S(2)}) collective-permute-start(f16[1,512,512]{2,1,0:T(8,128)(2,1)S(1)} %fusion.10), channel_id=1, source_target_pairs={{0,16},{4,20},{8,24},{12,28},{16,0},{20,4},{24,8},{28,12},{1,17},{... | collective-permute-start | bytes 1572872 | tf_op jit(solution)/shard_map/ppermute | solution.py:271
  154.5 22.9 %collective-permute-start.15 = (bf16[8,4096]{1,0:T(8,128)(2,1)S(1)}, bf16[8,4096]{1,0:T(8,128)(2,1)S(1)}, u32[]{:S(2)}, u32[]{:S(2)}) collective-permute-start(bf16[8,4096]{1,0:T(8,128)(2,1)S(1)} %convolution_convert_fusion.1), channel_id=1, source_target_pairs={{0,16},{4,20},{8,24},{12,28},{16,0},{20,4},{24,8},{28,12},{1,17},{... | collective-permute-start | bytes 196616 | tf_op jit(solution)/shard_map/ppermute | solution.py:271
  188.8 19.9 %collective-permute-start.18 = (f16[512,512]{1,0:T(8,128)(2,1)}, f16[512,512]{1,0:T(8,128)(2,1)}, u32[]{:S(2)}, u32[]{:S(2)}) collective-permute-start(f16[512,512]{1,0:T(8,128)(2,1)} %get-tuple-element.120), channel_id=1, source_target_pairs={{0,4},{4,0},{8,12},{12,8},{16,20},{20,16},{24,28},{28,24},{1,5},{5... | collective-permute-start | bytes 1572872 | tf_op jit(solution)/shard_map/ppermute | solution.py:271
  189.6 22.9 %collective-permute-start.19 = (f16[512,512]{1,0:T(8,128)(2,1)}, f16[512,512]{1,0:T(8,128)(2,1)}, u32[]{:S(2)}, u32[]{:S(2)}) collective-permute-start(f16[512,512]{1,0:T(8,128)(2,1)} %get-tuple-element.120), channel_id=1, source_target_pairs={{0,8},{4,12},{8,0},{12,4},{16,24},{20,28},{24,16},{28,20},{1,9},{5... | collective-permute-start | bytes 1572872 | tf_op jit(solution)/shard_map/ppermute | solution.py:271
  189.8 22.7 %collective-permute-start.20 = (f16[512,512]{1,0:T(8,128)(2,1)}, f16[512,512]{1,0:T(8,128)(2,1)}, u32[]{:S(2)}, u32[]{:S(2)}) collective-permute-start(f16[512,512]{1,0:T(8,128)(2,1)} %get-tuple-element.120), channel_id=1, source_target_pairs={{0,16},{4,20},{8,24},{12,28},{16,0},{20,4},{24,8},{28,12},{1,17},{... | collective-permute-start | bytes 1572872 | tf_op jit(solution)/shard_map/ppermute | solution.py:271
  190.8 16.5 %collective-permute-start.21 = (bf16[32,4096]{1,0:T(8,128)(2,1)S(1)}, bf16[32,4096]{1,0:T(8,128)(2,1)}, u32[]{:S(2)}, u32[]{:S(2)}) collective-permute-start(bf16[32,4096]{1,0:T(8,128)(2,1)S(1)} %pad_maximum_fusion.9), channel_id=1, source_target_pairs={{0,4},{4,0},{8,12},{12,8},{16,20},{20,16},{24,28},{28,24},{1,5},{5... | collective-permute-start | bytes 786440 | tf_op jit(solution)/shard_map/ppermute | solution.py:271
  191.7 17.0 %collective-permute-start.23 = (f32[128,512]{1,0:T(8,128)S(1)}, f32[128,512]{1,0:T(8,128)S(1)}, u32[]{:S(2)}, u32[]{:S(2)}) collective-permute-start(f32[128,512]{1,0:T(8,128)S(1)} %constant_dynamic-slice_fusion.2), channel_id=1, source_target_pairs={{0,2},{1,3},{2,0},{3,1},{4,6},{5,7},{6,4},{7,5},{8,10},{9,11},{10,... | collective-permute-start | bytes 786440 | tf_op jit(solution)/shard_map/ppermute | solution.py:271
  212.5 20.7 %collective-permute-start.25 = (f16[512,512]{1,0:T(8,128)(2,1)}, f16[512,512]{1,0:T(8,128)(2,1)S(1)}, u32[]{:S(2)}, u32[]{:S(2)}) collective-permute-start(f16[512,512]{1,0:T(8,128)(2,1)} %collective-permute-done.20), channel_id=1, source_target_pairs={{0,4},{4,0},{8,12},{12,8},{16,20},{20,16},{24,28},{28,24},{1,5},{5... | collective-permute-start | bytes 1572872 | tf_op jit(solution)/shard_map/ppermute | solution.py:271
  213.2 20.1 %collective-permute-start.26 = (f16[512,512]{1,0:T(8,128)(2,1)}, f16[512,512]{1,0:T(8,128)(2,1)S(1)}, u32[]{:S(2)}, u32[]{:S(2)}) collective-permute-start(f16[512,512]{1,0:T(8,128)(2,1)} %collective-permute-done.20), channel_id=1, source_target_pairs={{0,8},{4,12},{8,0},{12,4},{16,24},{20,28},{24,16},{28,20},{1,9},{5... | collective-permute-start | bytes 1572872 | tf_op jit(solution)/shard_map/ppermute | solution.py:271
  216.5 16.8 %collective-permute-start.24 = (f16[512,512]{1,0:T(8,128)(2,1)}, f16[512,512]{1,0:T(8,128)(2,1)S(1)}, u32[]{:S(2)}, u32[]{:S(2)}) collective-permute-start(f16[512,512]{1,0:T(8,128)(2,1)} %collective-permute-done.19), channel_id=1, source_target_pairs={{0,4},{4,0},{8,12},{12,8},{16,20},{20,16},{24,28},{28,24},{1,5},{5... | collective-permute-start | bytes 1572872 | tf_op jit(solution)/shard_map/ppermute | solution.py:271
  228.5 35.6 %collective-permute-start.34 = (f32[128,512]{1,0:T(8,128)S(1)}, f32[128,512]{1,0:T(8,128)S(1)}, u32[]{:S(2)}, u32[]{:S(2)}) collective-permute-start(f32[128,512]{1,0:T(8,128)S(1)} %dynamic-slice_add_fusion.3), channel_id=1, source_target_pairs={{0,16},{4,20},{8,24},{12,28},{16,0},{20,4},{24,8},{28,12},{1,17},{... | collective-permute-start | bytes 786440 | tf_op jit(solution)/shard_map/ppermute | solution.py:271
  233.4 30.7 %collective-permute-start.31 = (f16[512,512]{1,0:T(8,128)(2,1)S(1)}, f16[512,512]{1,0:T(8,128)(2,1)S(1)}, u32[]{:S(2)}, u32[]{:S(2)}) collective-permute-start(f16[512,512]{1,0:T(8,128)(2,1)S(1)} %collective-permute-done.26), channel_id=1, source_target_pairs={{0,4},{4,0},{8,12},{12,8},{16,20},{20,16},{24,28},{28,24},{1,5},{5... | collective-permute-start | bytes 1572872 | tf_op jit(solution)/shard_map/ppermute | solution.py:271
  234.1 29.9 %collective-permute-start.33 = (f32[64,576]{1,0:T(8,128)S(1)}, f32[64,576]{1,0:T(8,128)S(1)}, u32[]{:S(2)}, u32[]{:S(2)}) collective-permute-start(f32[64,576]{1,0:T(8,128)S(1)} %add.527), channel_id=1, source_target_pairs={{0,16},{4,20},{8,24},{12,28},{16,0},{20,4},{24,8},{28,12},{1,17},{... | collective-permute-start | bytes 442376 | tf_op jit(solution)/shard_map/ppermute | solution.py:271
  238.7 25.4 %collective-permute-start.32 = (f32[64,512]{1,0:T(8,128)S(1)}, f32[64,512]{1,0:T(8,128)S(1)}, u32[]{:S(2)}, u32[]{:S(2)}) collective-permute-start(f32[64,512]{1,0:T(8,128)S(1)} %fusion.52), channel_id=1, source_target_pairs={{0,16},{4,20},{8,24},{12,28},{16,0},{20,4},{24,8},{28,12},{1,17},{... | collective-permute-start | bytes 393224 | tf_op jit(solution)/shard_map/ppermute | solution.py:271
  264.1 29.2 %collective-permute-start.37 = (f32[128,512]{1,0:T(8,128)S(1)}, f32[128,512]{1,0:T(8,128)S(1)}, u32[]{:S(2)}, u32[]{:S(2)}) collective-permute-start(f32[128,512]{1,0:T(8,128)S(1)} %add.530), channel_id=1, source_target_pairs={{0,8},{4,12},{8,0},{12,4},{16,24},{20,28},{24,16},{28,20},{1,9},{5... | collective-permute-start | bytes 786440 | tf_op jit(solution)/shard_map/ppermute | solution.py:271
  265.4 27.9 %collective-permute-start.36 = (f32[64,576]{1,0:T(8,128)S(1)}, f32[64,576]{1,0:T(8,128)S(1)}, u32[]{:S(2)}, u32[]{:S(2)}) collective-permute-start(f32[64,576]{1,0:T(8,128)S(1)} %add.529), channel_id=1, source_target_pairs={{0,8},{4,12},{8,0},{12,4},{16,24},{20,28},{24,16},{28,20},{1,9},{5... | collective-permute-start | bytes 442376 | tf_op jit(solution)/shard_map/ppermute | solution.py:271
  265.8 27.5 %collective-permute-start.35 = (f32[64,512]{1,0:T(8,128)S(1)}, f32[64,512]{1,0:T(8,128)S(1)}, u32[]{:S(2)}, u32[]{:S(2)}) collective-permute-start(f32[64,512]{1,0:T(8,128)S(1)} %add.528), channel_id=1, source_target_pairs={{0,8},{4,12},{8,0},{12,4},{16,24},{20,28},{24,16},{28,20},{1,9},{5... | collective-permute-start | bytes 393224 | tf_op jit(solution)/shard_map/ppermute | solution.py:271
  296.8 19.2 %collective-permute-start.38 = (f32[2,576,512]{2,1,0:T(8,128)}, f32[2,576,512]{2,1,0:T(8,128)}, u32[]{:S(2)}, u32[]{:S(2)}) collective-permute-start(f32[2,576,512]{2,1,0:T(8,128)} %pad_maximum_fusion.1), channel_id=1, source_target_pairs={{0,1},{1,0},{2,3},{3,2},{4,5},{5,4},{6,7},{7,6},{8,9},{9,8},{10,11... | collective-permute-start | bytes 7077896 | tf_op jit(solution)/shard_map/ppermute | solution.py:271
  301.6 14.3 %collective-permute-start.41 = (f32[128,512]{1,0:T(8,128)S(1)}, f32[128,512]{1,0:T(8,128)S(1)}, u32[]{:S(2)}, u32[]{:S(2)}) collective-permute-start(f32[128,512]{1,0:T(8,128)S(1)} %add.536), channel_id=1, source_target_pairs={{0,4},{4,0},{8,12},{12,8},{16,20},{20,16},{24,28},{28,24},{1,5},{5... | collective-permute-start | bytes 786440 | tf_op jit(solution)/shard_map/ppermute | solution.py:271
  302.4 13.5 %collective-permute-start.40 = (f32[64,576]{1,0:T(8,128)S(1)}, f32[64,576]{1,0:T(8,128)S(1)}, u32[]{:S(2)}, u32[]{:S(2)}) collective-permute-start(f32[64,576]{1,0:T(8,128)S(1)} %add.535), channel_id=1, source_target_pairs={{0,4},{4,0},{8,12},{12,8},{16,20},{20,16},{24,28},{28,24},{1,5},{5... | collective-permute-start | bytes 442376 | tf_op jit(solution)/shard_map/ppermute | solution.py:271
  333.0 29.4 %collective-permute-start.45 = (f16[1,512,512]{2,1,0:T(8,128)(2,1)}, f16[1,512,512]{2,1,0:T(8,128)(2,1)S(1)}, u32[]{:S(2)}, u32[]{:S(2)}) collective-permute-start(f16[1,512,512]{2,1,0:T(8,128)(2,1)} %multiply_convert_fusion.2), channel_id=1, source_target_pairs={{0,2},{1,3},{2,0},{3,1},{4,6},{5,7},{6,4},{7,5},{8,10},{9,11},{10,... | collective-permute-start | bytes 1572872 | tf_op jit(solution)/shard_map/ppermute | solution.py:271
  333.5 28.8 %collective-permute-start.46 = (f32[1,64,512]{2,1,0:T(8,128)}, f32[1,64,512]{2,1,0:T(8,128)}, u32[]{:S(2)}, u32[]{:S(2)}) collective-permute-start(f32[1,64,512]{2,1,0:T(8,128)} %slice.190), channel_id=1, source_target_pairs={{0,2},{1,3},{2,0},{3,1},{4,6},{5,7},{6,4},{7,5},{8,10},{9,11},{10,... | collective-permute-start | bytes 393224 | tf_op jit(solution)/shard_map/ppermute | solution.py:271
  379.3 25.6 %collective-permute-start.49 = (f32[512,512]{1,0:T(8,128)S(1)}, f32[512,512]{1,0:T(8,128)S(1)}, u32[]{:S(2)}, u32[]{:S(2)}) collective-permute-start(f32[512,512]{1,0:T(8,128)S(1)} %fusion.53), channel_id=1, source_target_pairs={{0,2},{1,3},{2,0},{3,1},{4,6},{5,7},{6,4},{7,5},{8,10},{9,11},{10,... | collective-permute-start | bytes 3145736 | tf_op jit(solution)/shard_map/ppermute | solution.py:271
  406.6 16.4 %collective-permute-start.55 = (f32[2,512,512]{2,1,0:T(8,128)}, f32[2,512,512]{2,1,0:T(8,128)}, u32[]{:S(2)}, u32[]{:S(2)}) collective-permute-start(f32[2,512,512]{2,1,0:T(8,128)} %pad_maximum_fusion.2), channel_id=1, source_target_pairs={{0,1},{1,0},{2,3},{3,2},{4,5},{5,4},{6,7},{7,6},{8,9},{9,8},{10,11... | collective-permute-start | bytes 6291464 | tf_op jit(solution)/shard_map/ppermute | solution.py:271
  (51 other events, 331.0 us)
